TPU v7x, 128 devices: a whole 4x4x4 slice. The times are simulated.
128 devices in a mesh: kv: 4 (over x_lo, core), grp: 8 (over x_hi, z), prompt: 4 (over y).
Axes of the slice: x: 4 (x_hi: 2, x_lo: 2; x = x_hi * 2 + x_lo), y: 4, z: 4, core: 2. Of those that a mesh axis runs over, the one named last changes fastest.
Arguments:
- queries: bfloat16 [4, 8, 256, 8192], P('prompt', 'grp', None, 'kv'), may hold values from -6 to 6
- resp_keys: bfloat16 [4, 8, 256, 1024], P('prompt', 'grp', None, 'kv'), may hold values from -6 to 6
- resp_values: bfloat16 [4, 8, 256, 1024], P('prompt', 'grp', None, 'kv'), may hold values from -6 to 6
- prompt_keys: bfloat16 [4, 2048, 1024], P('prompt', ('kv', 'grp')), may hold values from -6 to 6
- prompt_values: bfloat16 [4, 2048, 1024], P('prompt', ('kv', 'grp')), may hold values from -6 to 6
- grad_out: bfloat16 [4, 8, 256, 8192], P('prompt', 'grp', None, 'kv'), may hold values from -6 to 6
- resp_len: int32 [4, 8], P('prompt', 'grp'), may hold values from 32 to 255, as said below
- prompt_len: int32 [4], P('prompt'), may hold values from 512 to 2048, as said below
Outputs:
- attended: bfloat16 [4, 8, 256, 8192], P('prompt', 'grp', None, 'kv')
- grad_queries: bfloat16 [4, 8, 256, 8192], P('prompt', 'grp', None, 'kv')
- grad_resp_keys: bfloat16 [4, 8, 256, 1024], P('prompt', 'grp', None, 'kv')
- grad_resp_values: bfloat16 [4, 8, 256, 1024], P('prompt', 'grp', None, 'kv')
- grad_prompt_keys: float32 [4, 2048, 1024], P('prompt', ('kv', 'grp'))
- grad_prompt_values: float32 [4, 2048, 1024], P('prompt', ('kv', 'grp'))
Inputs may be any that keep to these rules, and one draw needn't show every extreme that they name: `resp_len`: some response has exactly 255 valid tokens in every draw. `prompt_len`: some prompt has exactly 2048 valid tokens in every draw.
All inputs are finite; a program needn't handle non-finite values.
Results may differ from a plain program's by a relative error of at most 0.034.
Values may be sent and summed in bfloat16 or wider, within the bound.
A program may use at most 128 MiB of HBM per device.

v0:
```python
import jax
import jax.numpy as jnp
from jax import lax
from jax.sharding import PartitionSpec as P

HD = 128
QPG = 8


def guarded(compute, operand):
    result = compute(operand)
    return result


def on_device(
    queries, resp_keys, resp_values, prompt_keys, prompt_values, grad_out, resp_len, prompt_len
):
    scale = HD ** (-0.5)
    resp_dev = queries.shape[1]
    slice_len = queries.shape[2]
    kv_local = queries.shape[3] // (HD * QPG)
    row_count = resp_dev * slice_len
    valid_total = lax.psum(jnp.sum(resp_len).astype(jnp.float32), ("grp", "prompt"))
    slot_total = resp_dev * slice_len * lax.axis_size("grp") * lax.axis_size("prompt")
    weight = slot_total / valid_total
    whole_keys, whole_values = (
        lax.all_gather(prompt_keys, ("kv", "grp"), axis=1, tiled=True),
        lax.all_gather(prompt_values, ("kv", "grp"), axis=1, tiled=True),
    )
    head_start = lax.axis_index("kv") * (kv_local * HD)
    keys_here = lax.dynamic_slice_in_dim(whole_keys, head_start, kv_local * HD, 2)
    values_here = lax.dynamic_slice_in_dim(whole_values, head_start, kv_local * HD, 2)
    prompt_total = keys_here.shape[1]
    block = min(512, prompt_total)
    block_count = prompt_total // block
    key_blocks = keys_here.reshape(block_count, block, kv_local, HD)
    value_blocks = values_here.reshape(block_count, block, kv_local, HD)
    block_ids = jnp.arange(block_count)
    limit = prompt_len[0]
    lengths = resp_len[0]
    query_mat = queries.reshape(row_count, kv_local, QPG, HD)
    query_resp = queries.reshape(resp_dev, slice_len, kv_local, QPG, HD)
    key_resp = resp_keys.reshape(resp_dev, slice_len, kv_local, HD)
    value_resp = resp_values.reshape(resp_dev, slice_len, kv_local, HD)

    def prompt_scores(key_block, block_start):
        scores = (
            jnp.einsum("rkgd,jkd->kgrj", query_mat, key_block, preferred_element_type=jnp.float32)
            * scale
        )
        live = block_start + jnp.arange(block) < limit
        return (scores, live)

    slot_ids = jnp.arange(slice_len)
    resp_visible = (slot_ids[None, :] <= slot_ids[:, None])[None] & (
        slot_ids[None, None, :] < lengths[:, None, None]
    )
    resp_scores = (
        jnp.einsum("rskgd,rtkd->kgrst", query_resp, key_resp, preferred_element_type=jnp.float32)
        * scale
    )
    resp_masked = jnp.where(resp_visible, resp_scores, -jnp.inf)

    def stat_step(carry, item):
        key_block, index = item
        block_start = index * block

        def compute(state):
            scores, live = prompt_scores(key_block, block_start)
            masked = jnp.where(live, scores, -jnp.inf)
            new_high = jnp.maximum(state[0], jnp.max(masked, -1))
            new_sum = state[1] * jnp.exp(state[0] - new_high) + jnp.sum(
                jnp.exp(masked - new_high[..., None]), -1
            )
            return (new_high, new_sum)

        return (guarded(compute, carry), None)

    start_high = jnp.full((kv_local, QPG, row_count), -1e30, jnp.float32)
    start_sum = jnp.zeros((kv_local, QPG, row_count), jnp.float32)
    (prompt_high, prompt_sum), unused = lax.scan(
        stat_step, (start_high, start_sum), (key_blocks, block_ids)
    )
    resp_high = jnp.max(resp_masked, -1).reshape(kv_local, QPG, row_count)
    final_high = jnp.maximum(prompt_high, resp_high)
    final_shaped = final_high.reshape(kv_local, QPG, resp_dev, slice_len)
    resp_sum = jnp.sum(jnp.exp(resp_masked - final_shaped[..., None]), -1).reshape(
        kv_local, QPG, row_count
    )
    log_total = final_high + jnp.log(prompt_sum * jnp.exp(prompt_high - final_high) + resp_sum)
    log_resp = log_total.reshape(kv_local, QPG, resp_dev, slice_len)[..., None]

    def out_step(carry, item):
        key_block, value_block, index = item
        block_start = index * block

        def compute(accum):
            scores, live = prompt_scores(key_block, block_start)
            probs = jnp.exp(jnp.where(live, scores - log_total[..., None], -jnp.inf)).astype(
                jnp.bfloat16
            )
            return accum + jnp.einsum(
                "kgrj,jkd->rkgd", probs, value_block, preferred_element_type=jnp.float32
            )

        return (guarded(compute, carry), None)

    zero_rows = jnp.zeros((row_count, kv_local, QPG, HD), jnp.float32)
    prompt_part, unused = lax.scan(out_step, zero_rows, (key_blocks, value_blocks, block_ids))
    resp_probs = jnp.exp(jnp.where(resp_visible, resp_scores - log_resp, -jnp.inf)).astype(
        jnp.bfloat16
    )
    resp_part = jnp.einsum(
        "kgrst,rtkd->rskgd", resp_probs, value_resp, preferred_element_type=jnp.float32
    )
    attended = (prompt_part + resp_part.reshape(row_count, kv_local, QPG, HD)).astype(jnp.bfloat16)
    live_rows = (slot_ids[None, :] < lengths[:, None]).reshape(row_count).astype(jnp.float32)
    scaled = (
        grad_out.reshape(row_count, kv_local, QPG, HD).astype(jnp.float32)
        * live_rows[:, None, None, None]
        * weight
    ).astype(jnp.bfloat16)
    delta = jnp.sum(scaled.astype(jnp.float32) * attended.astype(jnp.float32), -1).transpose(
        1, 2, 0
    )
    scaled_resp = scaled.reshape(resp_dev, slice_len, kv_local, QPG, HD)
    delta_resp = delta.reshape(kv_local, QPG, resp_dev, slice_len)[..., None]

    def grad_step(carry, item):
        key_block, value_block, index = item
        block_start = index * block

        def compute(accum):
            scores, live = prompt_scores(key_block, block_start)
            probs = jnp.exp(jnp.where(live, scores - log_total[..., None], -jnp.inf)).astype(
                jnp.bfloat16
            )
            grad_probs = jnp.einsum(
                "rkgd,jkd->kgrj", scaled, value_block, preferred_element_type=jnp.float32
            )
            grad_scores = (
                probs.astype(jnp.float32) * (grad_probs - delta[..., None]) * scale
            ).astype(jnp.bfloat16)
            new_accum = accum + jnp.einsum(
                "kgrj,jkd->rkgd", grad_scores, key_block, preferred_element_type=jnp.float32
            )
            key_grad = jnp.einsum(
                "kgrj,rkgd->jkd", grad_scores, query_mat, preferred_element_type=jnp.float32
            )
            value_grad = jnp.einsum(
                "kgrj,rkgd->jkd", probs, scaled, preferred_element_type=jnp.float32
            )
            return (new_accum, key_grad, value_grad)

        new_accum, key_grad, value_grad = guarded(compute, carry)
        return (new_accum, (key_grad, value_grad))

    query_accum, (key_grads, value_grads) = lax.scan(
        grad_step, zero_rows, (key_blocks, value_blocks, block_ids)
    )
    resp_grad_probs = jnp.einsum(
        "rskgd,rtkd->kgrst", scaled_resp, value_resp, preferred_element_type=jnp.float32
    )
    resp_grad_scores = (
        resp_probs.astype(jnp.float32) * (resp_grad_probs - delta_resp) * scale
    ).astype(jnp.bfloat16)
    resp_query_grad = jnp.einsum(
        "kgrst,rtkd->rskgd", resp_grad_scores, key_resp, preferred_element_type=jnp.float32
    )
    grad_queries = (query_accum + resp_query_grad.reshape(row_count, kv_local, QPG, HD)).astype(
        jnp.bfloat16
    )
    grad_resp_keys = jnp.einsum(
        "kgrst,rskgd->rtkd", resp_grad_scores, query_resp, preferred_element_type=jnp.float32
    )
    grad_resp_values = jnp.einsum(
        "kgrst,rskgd->rtkd", resp_probs, scaled_resp, preferred_element_type=jnp.float32
    )
    partial_keys = key_grads.reshape(1, prompt_total, kv_local * HD)
    partial_values = value_grads.reshape(1, prompt_total, kv_local * HD)
    spread_keys, spread_values = (
        lax.all_to_all(partial_keys, "kv", split_axis=1, concat_axis=2, tiled=True),
        lax.all_to_all(partial_values, "kv", split_axis=1, concat_axis=2, tiled=True),
    )
    grad_prompt_keys, grad_prompt_values = (
        lax.psum_scatter(spread_keys, "grp", scatter_dimension=1, tiled=True),
        lax.psum_scatter(spread_values, "grp", scatter_dimension=1, tiled=True),
    )
    return (
        attended.reshape(queries.shape),
        grad_queries.reshape(queries.shape),
        grad_resp_keys.astype(jnp.bfloat16).reshape(resp_keys.shape),
        grad_resp_values.astype(jnp.bfloat16).reshape(resp_values.shape),
        grad_prompt_keys,
        grad_prompt_values,
    )


def solution(mesh):
    placed = (
        P("prompt", "grp", None, "kv"),
        P("prompt", "grp", None, "kv"),
        P("prompt", "grp", None, "kv"),
        P("prompt", ("kv", "grp"), None),
        P("prompt", ("kv", "grp"), None),
        P("prompt", "grp", None, "kv"),
        P("prompt", "grp"),
        P("prompt"),
    )
    return jax.shard_map(
        on_device,
        mesh=mesh,
        in_specs=placed,
        out_specs=(
            P("prompt", "grp", None, "kv"),
            P("prompt", "grp", None, "kv"),
            P("prompt", "grp", None, "kv"),
            P("prompt", "grp", None, "kv"),
            P("prompt", ("kv", "grp"), None),
            P("prompt", ("kv", "grp"), None),
        ),
        check_vma=False,
    )
```

profile of v0, /device:TPU:1, one launch (start us, length us, event | category | flops | bytes accessed | tf_op | source)
XLA Modules:
  0.0 521.4 jit_solution(17743768807684745512)
XLA Ops:
  9.3 85.2 %psum.7 = f32[]{:T(128)} all-reduce(f32[]{:T(128)S(6)} %convert_element_type.84), channel_id=1, replica_groups=mesh['kv'=4,'grp'=8,'prompt'=4] {'grp','prompt'}, use_global_device_ids=true, to_apply=%region_8.9 | all-reduce | flops 1 | bytes 8 | tf_op jit(solution)/shard_map/psum | solution.py:23
  104.4 4.0 fusion.44
  115.1 74.5 %all-gather.3.cloned.1.call-done = bf16[1,2048,1024]{2,1,0:T(8,128)(2,1)} async-done(((bf16[1,64,1024]{2,1,0:T(8,128)(2,1)}), bf16[1,2048,1024]{2,1,0:T(8,128)(2,1)}) %all-gather.3.cloned.1.call-update) | async-done | bytes 4194320 | tf_op jit(solution)/shard_map/all_gather | solution.py:28
  193.9 24.6 %while.39 = (s32[]{:T(128)}, f32[2,8,256]{2,1,0:T(8,128)S(1)}, f32[2,8,256]{2,1,0:T(8,128)S(1)}, s32[4]{0:T(128)S(1)}, s32[]{:T(128)}, /*index=5*/bf16[4,512,2,1...) while((s32[]{:T(128)}, f32[2,8,256]{2,1,0:T(8,128)S(1)}, ...), condition=%wide.region_3.4_spmd.clone, body=%wide.region_0.3_spmd.clone.sunk | while | flops 551572480 | bytes 18302620 | solution.py:81
  218.6 3.2 exponential_reduce_fusion
  224.1 39.7 %while.40 = (s32[]{:T(128)}, f32[256,2,8,128]{0,3,2,1:T(8,128)}, bf16[4,512,2,128]{3,2,1,0:T(2,128)(2,1)}, s32[4]{0:T(128)S(1)}, s32[]{:T(128)}, /*index=5*/bf16...) while((s32[]{:T(128)}, f32[256,2,8,128]{0,3,2,1:T(8,128)}, ...), condition=%wide.region_7.8_spmd.clone, body=%wide.region_6.7_spmd.clone.sunk | while | flops 1083180032 | bytes 6833503 | solution.py:109
  228.6 4.9 bitcast_add_fusion.6
  237.9 5.7 %bitcast_add_fusion.6 = f32[256,2,8,128]{0,3,2,1:T(8,128)} fusion(f32[256,2,8,128]{0,3,2,1:T(8,128)} %get-tuple-element.653, f32[2,8,256]{2,1,0:T(8,128)S(1)} %get-tuple-element.670, pred[512]{0:T(512)(128)(4,1)} %add_compare_fusion.7, bf16[256,2,8,128]{3,0,2,1:T(8,128)(2,1)S(1)} %get-tuple-element.669, pred[]{:T(512)S(6)} %compare.10, ...), kind=kOutput, calls=%fused_computation.20.clone.1 | convolution fusion | flops 1083179008 | bytes 5784069 | tf_op jit(solution)/shard_map/while/body/eval_jaxpr/kgrj,jkd->rkgd/dot_general | solution.py:102
  248.0 5.7 %bitcast_add_fusion.6 = f32[256,2,8,128]{0,3,2,1:T(8,128)} fusion(f32[256,2,8,128]{0,3,2,1:T(8,128)} %get-tuple-element.653, f32[2,8,256]{2,1,0:T(8,128)S(1)} %get-tuple-element.670, pred[512]{0:T(512)(128)(4,1)} %add_compare_fusion.7, bf16[256,2,8,128]{3,0,2,1:T(8,128)(2,1)S(1)} %get-tuple-element.669, pred[]{:T(512)S(6)} %compare.10, ...), kind=kOutput, calls=%fused_computation.20.clone.1 | convolution fusion | flops 1083179008 | bytes 5784069 | tf_op jit(solution)/shard_map/while/body/eval_jaxpr/kgrj,jkd->rkgd/dot_general | solution.py:102
  258.1 5.7 %bitcast_add_fusion.6 = f32[256,2,8,128]{0,3,2,1:T(8,128)} fusion(f32[256,2,8,128]{0,3,2,1:T(8,128)} %get-tuple-element.653, f32[2,8,256]{2,1,0:T(8,128)S(1)} %get-tuple-element.670, pred[512]{0:T(512)(128)(4,1)} %add_compare_fusion.7, bf16[256,2,8,128]{3,0,2,1:T(8,128)(2,1)S(1)} %get-tuple-element.669, pred[]{:T(512)S(6)} %compare.10, ...), kind=kOutput, calls=%fused_computation.20.clone.1 | convolution fusion | flops 1083179008 | bytes 5784069 | tf_op jit(solution)/shard_map/while/body/eval_jaxpr/kgrj,jkd->rkgd/dot_general | solution.py:102
  263.8 4.9 multiply_reduce_fusion
  271.0 56.5 %while.41 = (s32[]{:T(128)}, f32[256,2,8,128]{0,3,2,1:T(8,128)S(1)}, f32[4,512,2,128]{3,2,1,0:T(2,128)}, f32[4,512,2,128]{3,2,1,0:T(2,128)}, bf16[4,512,2,128]{3...) while((s32[]{:T(128)}, ...), condition=%wide.region_11.12_spmd.clone, body=%wide.region_10.11_spmd.clone.sunk | while | flops 2704278528 | bytes 42239208 | solution.py:158
  274.0 3.0 fusion.124
  288.2 3.0 fusion.124
  302.3 3.0 fusion.124
  316.4 3.0 fusion.124
  327.5 29.4 %all_to_all.36 = f32[1,2048,256]{2,0,1:T(1,128)} all-to-all(f32[1,2048,256]{2,0,1:T(1,128)} %bitcast.294), channel_id=1, replica_groups=mesh['kv'=4,'grp'=8,'prompt'=4] {'kv'}, dimensions={1} | all-to-all | bytes 4194304 | tf_op jit(solution)/shard_map/all_to_all | solution.py:183
  356.9 5.5 %all-to-all-start = ((f32[1,2048,256]{2,0,1:T(1,128)}), f32[1,2048,256]{2,0,1:T(1,128)}, u32[]{:S(2)}, u32[]{:S(2)}) async-start(f32[1,2048,256]{2,0,1:T(1,128)} %bitcast.295), calls=%async_computation | async-start | bytes 4194304 | tf_op jit(solution)/shard_map/all_to_all | solution.py:182
  362.4 3.1 copy.179
  368.4 6.1 %copy.132 = f32[1,512,1024]{2,0,1:T(1,128)} copy(f32[1,512,1024]{1,2,0:T(8,128)} %bitcast.289) | data formatting | bytes 4194304 | tf_op jit(solution)/shard_map/all_to_all | solution.py:183
  374.5 12.8 %all-to-all-done = f32[1,2048,256]{2,0,1:T(1,128)} async-done(((f32[1,2048,256]{2,0,1:T(1,128)}), f32[1,2048,256]{2,0,1:T(1,128)}, u32[]{:S(2)}, u32[]{:S(2)}) %all-to-all-start) | async-done | bytes 2097184 | tf_op jit(solution)/shard_map/all_to_all | solution.py:182
  387.3 3.1 copy.178
  393.3 6.1 %copy.128 = f32[1,512,1024]{2,0,1:T(1,128)} copy(f32[1,512,1024]{1,2,0:T(8,128)} %bitcast.291) | data formatting | bytes 4194304 | tf_op jit(solution)/shard_map/all_to_all | solution.py:182
  415.0 96.5 %all-reduce.5.cloned.1.call-done = (f32[1,512,1024]{2,0,1:T(1,128)}, f32[1,512,1024]{2,0,1:T(1,128)}) async-done(((f32[1,512,1024]{2,0,1:T(1,128)}, f32[1,512,1024]{2,0,1:T(1,128)}), (f32[1,512,1024]{2,0,1:T(1,128)}, f32[1,512,1024]{2,0,1:T(1,128)})) %all-reduce.5.cloned.1.call-update) | async-done | bytes 4194320
  (162 shorter events, 129.1 us)
Async XLA Ops:
  7.2 101.2 %all-gather.5.cloned.1.call-start = ((), (), s32[]{:S(2)}) async-start(), calls=%async_computation.3 | async-start | bytes 4325376 | tf_op jit(solution)/shard_map/all_gather | solution.py:27
  7.9 181.6 %all-gather.3.cloned.1.call-start = ((), (), s32[]{:S(2)}) async-start(), calls=%async_computation.2 | async-start | bytes 4325376 | tf_op jit(solution)/shard_map/all_gather | solution.py:28
  95.5 12.8 %copy-start.5 = (bf16[256,2,128,1]{0,2,3,1:T(8,128)(2,1)}, bf16[256,2,128,1]{0,2,3,1:T(8,128)(2,1)S(1)}, u32[]{:S(2)}) copy-start(bf16[256,2,128,1]{0,2,3,1:T(8,128)(2,1)S(1)} %copy.157) | copy-start | bytes 393220
  218.5 3.5 copy-start
  224.1 2.4 copy-start.8
  228.6 4.9 copy-start.9
  233.5 2.4 copy-start.8
  237.9 5.7 %copy-start.9 = (s32[4]{0:T(128)S(1)}, s32[4]{0:T(128)}, u32[]{:S(2)}) copy-start(s32[4]{0:T(128)} %copy-done.8) | copy-start | bytes 52 | tf_op jit(solution)/shard_map/while
  243.6 2.4 copy-start.8
  248.0 5.7 %copy-start.9 = (s32[4]{0:T(128)S(1)}, s32[4]{0:T(128)}, u32[]{:S(2)}) copy-start(s32[4]{0:T(128)} %copy-done.8) | copy-start | bytes 52 | tf_op jit(solution)/shard_map/while
  253.7 2.4 copy-start.8
  258.1 5.7 %copy-start.9 = (s32[4]{0:T(128)S(1)}, s32[4]{0:T(128)}, u32[]{:S(2)}) copy-start(s32[4]{0:T(128)} %copy-done.8) | copy-start | bytes 52 | tf_op jit(solution)/shard_map/while
  274.0 3.0 copy-start.1
  288.2 3.0 copy-start.1
  302.3 3.0 copy-start.1
  316.4 3.0 copy-start.1
  356.9 30.4 %all-to-all-start = ((f32[1,2048,256]{2,0,1:T(1,128)}), f32[1,2048,256]{2,0,1:T(1,128)}, u32[]{:S(2)}, u32[]{:S(2)}) async-start(f32[1,2048,256]{2,0,1:T(1,128)} %bitcast.295), calls=%async_computation | async-start | bytes 4194304 | tf_op jit(solution)/shard_map/all_to_all | solution.py:182
  362.4 149.1 %all-reduce.5.cloned.1.call-start = ((), (), s32[]{:S(2)}) async-start(), calls=%async_computation.4 | async-start | bytes 8388608
  393.3 6.1 %copy-start.7 = (u32[128]{0:T(128)S(1)}, u32[128]{0:T(128)}, u32[]{:S(2)}) copy-start(u32[128]{0:T(128)} %constant.82) | copy-start | bytes 1540
  399.4 3.5 copy-start.3
  403.0 3.8 copy-start.4
  405.4 1.3 copy-start.2
  406.8 4.7 copy-start.6
Sparse Core Ops, SparseCore 0:
  9.7 90.4 all-gather.4
  101.8 87.6 all-gather.2
  399.6 111.8 all-reduce.4
where the time goes:
time: 524 us; the launch traced here: 521 us
  waiting for transfers between devices  185 us (35%)
  blocking collectives  115 us (22%)
  matrix products  84.4 us (16%)
  local copies, waits for them, and re-layouts  83.8 us (16%)
  other arithmetic  23.8 us (5%)
  between operations  15.9 us (3%)
  loops' own time  8.3 us (2%)
  starting transfers between devices  5.53 us (1%)
    unnamed x4, waiting for transfers between devices  97.8 us
    psum x1, blocking collectives, on_device(): lax.psum(jnp.sum(resp_len).astype(jnp.float32), ('grp', 'prompt'))  85.2 us
    all_gather x1, waiting for transfers between devices, on_device(): lax.all_gather(prompt_values, ('kv', 'grp'), axis=1, tiled=True)  74.5 us
    all_to_all x1, blocking collectives, on_device(): lax.all_to_all(partial_values, 'kv', split_axis=1, concat_axis=2, tiled=T...  29.4 us
    unnamed x29, local copies, waits for them, and re-layouts  25.4 us
    dot_general x4, matrix products, compute(): jnp.einsum('kgrj,jkd->rkgd', probs, value_block, preferred_element_type=j...  22 us
    dot_general x8, matrix products, prompt_scores(): jnp.einsum('rkgd,jkd->kgrj', query_mat, key_block, preferred_element_type...  20.8 us
    dynamic_slice x24, local copies, waits for them, and re-layouts, on_device(): lax.scan(stat_step, (start_high, start_sum), (key_blocks, block_ids))  19.6 us
  transfers between devices with their start and end apart: 4, of which 3 were waited for; matrix products, arithmetic and copies ran while one was open for 9% of the time, Pallas kernels for 0%

commit v1 on v0

v1 whole, which is shorter than its diff:
```python
import functools

import jax
import jax.numpy as jnp
from jax import lax
from jax.experimental import pallas as pl
from jax.experimental.pallas import tpu as pltpu
from jax.sharding import PartitionSpec as P

F32 = jnp.float32
BF = jnp.bfloat16
MESH = pl.DeviceIdType.MESH
HD = 128
QPG = 8
SCALE = HD ** (-0.5)
LOG2E = 1.4426950408889634
NT = (((1,), (1,)), ((), ()))
NN = (((1,), (0,)), ((), ()))
SET = 256
PC = 512
HEADS = 16
SLOTS = 256
SETS = ((0, 0), (0, 3), (0, 1), (1, 0), (1, 1), (1, 3), (0, 2), (1, 2))


def dot(a, b, dims):
    return lax.dot_general(a, b, dims, preferred_element_type=F32)


def cat(parts, axis):
    return parts[0] if len(parts) == 1 else jnp.concatenate(parts, axis)


def kernel(
    rl_ref, pl_ref, q_ref, do_ref, rk_ref, rv_ref, pk_ref, pv_ref,
    o_ref, dq_ref, drk_ref, drv_ref, dpk_ref, dpv_ref,
    sets, p_ref, o_acc, dq_acc, mc, lse, ka, va, k_t, v_t, qq, dd, s_a, s_b,
    dk_acc, dv_acc, out_buf, half_in, full_in, x_in, fin, w_own, w_in,
    a2a_s, a2a_r, gs, gr, hs, hr, fs, fr, xs, xr, ks, kr, ws, wr,
):
    kv = lax.axis_index("kv")
    grp = lax.axis_index("grp")
    prm = lax.axis_index("prompt")
    xh = grp // 4
    z = grp % 4
    zat = lambda d: {"grp": xh * 4 + (z + d) % 4}
    zp, zm, xp = zat(1), zat(3), {"grp": (1 - xh) * 4 + z}
    kvat = lambda d: (kv + d) % 4
    yat = lambda d: {"prompt": (prm + d) % 4}

    peers = [{"kv": kvat(d)} for d in (1, 2, 3)] + [zat(d) for d in (1, 2, 3)]
    peers += [yat(d) for d in (1, 2, 3)] + [xp]
    barrier = pltpu.get_barrier_semaphore()
    for peer in peers:
        pl.semaphore_signal(barrier, inc=1, device_id=peer, device_id_type=MESH)
    pl.semaphore_wait(barrier, len(peers))

    def cp(src, dst, ssem, rsem, dev):
        return pltpu.make_async_remote_copy(
            src_ref=src, dst_ref=dst, send_sem=ssem, recv_sem=rsem, device_id=dev, device_id_type=MESH
        )

    spread = []
    for d in (1, 2, 3):
        cols = pl.ds(pl.multiple_of(kvat(d) * 256, 256), 256)
        rows = pl.ds(pl.multiple_of(kv * 64, 64), 64)
        for t, ref in ((0, pk_ref), (1, pv_ref)):
            i = (d - 1) * 2 + t
            spread.append(cp(ref.at[:, cols], sets.at[0, t, rows, :], a2a_s.at[i], a2a_r.at[i], {"kv": kvat(d)}))
    lo, hi = pl.ds(0, 128), pl.ds(128, 128)
    to_x = cp(sets.at[0], sets.at[3], gs.at[0], gr.at[0], xp)
    to_p = cp(sets.at[0], sets.at[1], gs.at[1], gr.at[1], zp)
    to_m = cp(sets.at[0], sets.at[2], gs.at[2], gr.at[2], zm)
    on_p = cp(sets.at[1, :, lo], sets.at[6, :, lo], gs.at[3], gr.at[3], zp)
    on_m = cp(sets.at[2, :, hi], sets.at[6, :, hi], gs.at[4], gr.at[4], zm)
    xto_p = cp(sets.at[3], sets.at[5], gs.at[5], gr.at[5], zp)
    xto_m = cp(sets.at[3], sets.at[4], gs.at[6], gr.at[6], zm)
    xon_p = cp(sets.at[5, :, lo], sets.at[7, :, lo], gs.at[7], gr.at[7], zp)
    xon_m = cp(sets.at[4, :, hi], sets.at[7, :, hi], gs.at[8], gr.at[8], zm)
    gather = [to_x, to_p, to_m, on_p, on_m, xto_p, xto_m, xon_p, xon_m]
    w_x = cp(w_own.at[0], w_in.at[0], ws.at[0], wr.at[0], xp)
    w_z = [cp(w_own.at[1], w_in.at[d], ws.at[d], wr.at[d], zat(d)) for d in (1, 2, 3)]
    w_y = [cp(w_own.at[2], w_in.at[3 + d], ws.at[3 + d], wr.at[3 + d], yat(d)) for d in (1, 2, 3)]
    half = {}
    full = {}
    for dx, s in ((0, 6), (1, 7)):
        half[dx, 0] = cp(out_buf.at[s, :, lo], half_in.at[dx, 0], hs.at[dx * 2], hr.at[dx * 2], zp)
        half[dx, 1] = cp(out_buf.at[s, :, hi], half_in.at[dx, 1], hs.at[dx * 2 + 1], hr.at[dx * 2 + 1], zm)
    for dx, d, s in ((0, 0, 2), (0, 1, 1), (1, 0, 4), (1, 1, 5)):
        i = dx * 2 + d
        full[dx, d] = cp(out_buf.at[s], full_in.at[dx, d], fs.at[i], fr.at[i], zm if d else zp)
    sum_x = cp(out_buf.at[3], x_in, xs, xr, xp)
    owners = []
    for d in (1, 2, 3):
        rows = pl.ds(pl.multiple_of(kvat(d) * 64, 64), 64)
        owners.append(cp(out_buf.at[0, :, rows, :], fin.at[d], ks.at[d], kr.at[d], {"kv": kvat(d)}))

    for c in spread:
        c.start()
    w_own[0] = jnp.full((8, 128), rl_ref[0, 0].astype(F32))
    w_x.start()

    rows = pl.ds(pl.multiple_of(kv * 64, 64), 64)
    cols = pl.ds(pl.multiple_of(kv * 256, 256), 256)
    sets[0, 0, rows, :] = pk_ref[:, cols]
    sets[0, 1, rows, :] = pv_ref[:, cols]

    live = lax.broadcasted_iota(jnp.int32, (SLOTS, HD), 0) < rl_ref[0, 0]

    def stage_queries(h, _):
        col = pl.ds(pl.multiple_of(h * HD, HD), HD)
        q = q_ref[:, col]
        qq[h, :, 0:HD] = q
        qq[h, :, HD:] = q
        dd[h, :, 0:HD] = jnp.where(live, do_ref[:, col].astype(F32), 0.0).astype(BF)
        return 0

    lax.fori_loop(0, HEADS, stage_queries, 0)
    ones = jnp.where(lax.broadcasted_iota(jnp.int32, (2304, HD), 1) < 2, 1.0, 0.0).astype(BF)
    for kh in range(2):
        va[kh, :, HD:] = ones

    def put_keys(kh, at, k, k_masked, v, valid):
        scaled = k * (SCALE * LOG2E)
        high = scaled.astype(BF)
        ka[kh, pl.ds(at, SET), 0:HD] = high
        ka[kh, pl.ds(at, SET), HD:] = (scaled - high.astype(F32)).astype(BF)
        va[kh, pl.ds(at, SET), 0:HD] = v.astype(BF)
        k_t[kh, :, pl.ds(at, SET)] = k_masked.T.astype(BF)
        v_t[kh, 0:HD, pl.ds(at, SET)] = v.T.astype(BF)
        v_t[kh, HD:, pl.ds(at, SET)] = valid

    for kh in range(2):
        k = rk_ref[:, kh * HD:(kh + 1) * HD].astype(F32)
        v = rv_ref[:, kh * HD:(kh + 1) * HD].astype(F32)
        put_keys(kh, 2048, k, k, v, jnp.ones((16, SET), BF))

    plen = pl_ref[0]

    def key_index(s, shape, axis):
        dx, dz = SETS[s]
        owner = (xh if dx == 0 else 1 - xh) * 4 + (z + dz) % 4
        r = lax.broadcasted_iota(jnp.int32, shape, axis)
        return ((r // 64) * 8 + owner) * 64 + r % 64

    def put_set(s):
        dead = key_index(s, (SET, HD), 0) >= plen
        valid = jnp.where(key_index(s, (16, SET), 1) < plen, 1.0, 0.0).astype(BF)
        for kh in range(2):
            k = sets[s, 0, :, kh * HD:(kh + 1) * HD].astype(F32)
            v = sets[s, 1, :, kh * HD:(kh + 1) * HD].astype(F32)
            put_keys(kh, s * SET, jnp.where(dead, k[0:1, :], k), jnp.where(dead, 0.0, k),
                     jnp.where(dead, 0.0, v), valid)

    def fwd_resp(h, _):
        kh = h // QPG
        s = dot(ka[kh, 2048:2304, :], qq[h], NT)
        t = lax.broadcasted_iota(jnp.int32, (SET, SLOTS), 0)
        i = lax.broadcasted_iota(jnp.int32, (SET, SLOTS), 1)
        s = jnp.where((t <= i) & (t < rl_ref[0, 0]), s, -1e30)
        m = jnp.max(s, 0, keepdims=True)
        p = jnp.exp2(s - m).astype(BF)
        mc[0, h] = m
        p_ref[h, 2048:2304, :] = p
        o_acc[h] = dot(v_t[kh, :, 2048:2304], p, NN)
        return 0

    for c in spread:
        c.wait_recv()
    for c in (to_x, to_p, to_m):
        c.start()
    lax.fori_loop(0, HEADS, fwd_resp, 0)
    w_x.wait_recv()
    w_own[1] = w_own[0] + w_in[0]
    for c in w_z:
        c.start()
    put_set(0)

    def score(c, at, h, s_ref):
        kh = h // QPG
        top = None
        for r in range(0, PC, 256):
            s = dot(ka[kh, pl.ds(at + r, 256), :], qq[h], NT)
            s_ref[r:r + 256, :] = s
            b = jnp.max(s.reshape(32, 8, SLOTS), 0)
            top = b if top is None else jnp.maximum(top, b)
        mc[c + 1, h] = jnp.maximum(mc[c, h], jnp.max(top, 0, keepdims=True))

    def attend(c, at, h, s_ref):
        kh = h // QPG
        m = mc[c + 1, h]
        old = o_acc[h] * jnp.exp2(mc[c, h] - m)
        parts = []
        for r in range(0, PC, 256):
            p = jnp.exp2(s_ref[r:r + 256, :] - m).astype(BF)
            p_ref[h, pl.ds(at + r, 256), :] = p
            parts.append(p)
        o_acc[h] = old + dot(v_t[kh, :, pl.ds(at, PC)], cat(parts, 0), NN)

    def fwd_chunk(c, _):
        @pl.when(c == 0)
        def _():
            to_p.wait_recv()
            on_p.start()
            to_m.wait_recv()
            on_m.start()
            put_set(1)

        @pl.when(c == 1)
        def _():
            to_x.wait_recv()
            xto_p.start()
            xto_m.start()
            put_set(2)
            put_set(3)
            for w in w_z:
                w.wait_recv()
            w_own[2] = w_own[1] + (w_in[1] + w_in[2] + w_in[3])
            for w in w_y:
                w.start()

        @pl.when(c == 2)
        def _():
            xto_p.wait_recv()
            xon_p.start()
            xto_m.wait_recv()
            xon_m.start()
            put_set(4)
            put_set(5)

        @pl.when(c == 3)
        def _():
            on_p.wait_recv()
            on_m.wait_recv()
            put_set(6)
            xon_p.wait_recv()
            xon_m.wait_recv()
            put_set(7)

        at = pl.multiple_of(c * PC, PC)
        score(c, at, 0, s_a)

        def heads(i, _):
            score(c, at, 2 * i + 1, s_b)
            attend(c, at, 2 * i, s_a)
            score(c, at, jnp.minimum(2 * i + 2, HEADS - 1), s_a)
            attend(c, at, 2 * i + 1, s_b)
            return 0

        lax.fori_loop(0, HEADS // 2, heads, 0)
        return 0

    lax.fori_loop(0, 4, fwd_chunk, 0)

    lane = lax.broadcasted_iota(jnp.int32, (SLOTS, HD), 1)

    def finish_fwd(h, _):
        col = pl.ds(pl.multiple_of(h * HD, HD), HD)
        o = o_acc[h]
        total = o[HD:HD + 1, :]
        out = (o[0:HD, :] * (1.0 / total)).T.astype(BF)
        o_ref[:, col] = out
        delta = -jnp.sum(out.astype(F32) * dd[h, :, 0:HD].astype(F32), 1, keepdims=True)
        high = delta.astype(BF).astype(F32)
        dd[h, :, HD:] = jnp.where(lane == 0, high, jnp.where(lane == 1, delta - high, 0.0)).astype(BF)
        lse[h] = mc[4, h] + jnp.log2(total)
        dq_acc[h] = jnp.zeros((HD, SLOTS), F32)
        return 0

    lax.fori_loop(0, HEADS, finish_fwd, 0)
    for w in w_y:
        w.wait_recv()
    count = w_own[2] + (w_in[4] + w_in[5] + w_in[6])
    weight = (8192.0 / count)[0:1, :]

    UB = 4

    def bwd_part(c, at, rows, kh):
        sub = min(256, rows)
        cols = slice(kh * HD, (kh + 1) * HD)
        dk_acc[0:rows, cols] = jnp.zeros((rows, HD), F32)
        dv_acc[0:rows, cols] = jnp.zeros((rows, HD), F32)

        def heads(i, _):
            ps, ss, dos, qs = [], [], [], []
            for u in range(UB):
                h = kh * QPG + i * UB + u
                corr = jnp.exp2(mc[c, h] - lse[h])
                pp, sp = [], []
                for r in range(0, rows, sub):
                    dp = dot(va[kh, pl.ds(at + r, sub), :], dd[h], NT)
                    p = p_ref[h, pl.ds(at + r, sub), :].astype(F32) * corr
                    pp.append(p.astype(BF))
                    sp.append((p * dp).astype(BF))
                ds = cat(sp, 0)
                dq_acc[h] += dot(k_t[kh, :, pl.ds(at, rows)], ds, NN)
                ps.append(cat(pp, 0))
                ss.append(ds)
                dos.append(dd[h, :, 0:HD])
                qs.append(qq[h, :, 0:HD])
            dv_acc[0:rows, cols] += dot(cat(ps, 1), cat(dos, 0), NN)
            dk_acc[0:rows, cols] += dot(cat(ss, 1), cat(qs, 0), NN)
            return 0

        lax.fori_loop(0, QPG // UB, heads, 0)

    def acc_of(s):
        r = (s % 2) * SET
        return dk_acc[r:r + SET, :], dv_acc[r:r + SET, :]

    def bwd_chunk(i, _):
        c = 3 - i
        at = pl.multiple_of(c * PC, PC)
        for kh in range(2):
            bwd_part(c + 1, at, PC, kh)

        @pl.when(c == 3)
        def _():
            for dx, s in ((1, 7), (0, 6)):
                for t, a in enumerate(acc_of(s)):
                    out_buf[s, t] = a.astype(BF)
                half[dx, 0].start()
                half[dx, 1].start()

        @pl.when(c == 2)
        def _():
            for d, s in ((0, 4), (1, 5)):
                half[1, d].wait_recv()
                for t, a in enumerate(acc_of(s)):
                    part = half_in[1, d, t].astype(F32)
                    out_buf[s, t, d * 128:d * 128 + 128, :] = (a[d * 128:d * 128 + 128] + part).astype(BF)
                    e = 1 - d
                    out_buf[s, t, e * 128:e * 128 + 128, :] = a[e * 128:e * 128 + 128].astype(BF)
                full[1, d].start()

        @pl.when(c == 1)
        def _():
            half[0, 0].wait_recv()
            for t, a in enumerate(acc_of(2)):
                out_buf[2, t, 0:128, :] = (a[0:128] + half_in[0, 0, t].astype(F32)).astype(BF)
                out_buf[2, t, 128:256, :] = a[128:256].astype(BF)
            full[0, 0].start()
            full[1, 0].wait_recv()
            full[1, 1].wait_recv()
            for t, a in enumerate(acc_of(3)):
                out_buf[3, t] = (a + full_in[1, 0, t].astype(F32) + full_in[1, 1, t].astype(F32)).astype(BF)
            sum_x.start()

        @pl.when(c == 0)
        def _():
            half[0, 1].wait_recv()
            for t, a in enumerate(acc_of(1)):
                out_buf[1, t, 0:128, :] = a[0:128].astype(BF)
                out_buf[1, t, 128:256, :] = (a[128:256] + half_in[0, 1, t].astype(F32)).astype(BF)
            full[0, 1].start()
            full[0, 0].wait_recv()
            full[0, 1].wait_recv()
            sum_x.wait_recv()
            for t, a in enumerate(acc_of(0)):
                more = full_in[0, 0, t].astype(F32) + full_in[0, 1, t].astype(F32) + x_in[t].astype(F32)
                out_buf[0, t] = (a + more).astype(BF)
            for o in owners:
                o.start()

        return 0

    lax.fori_loop(0, 4, bwd_chunk, 0)
    for kh in range(2):
        bwd_part(0, 2048, SET, kh)
    w2 = cat([weight, weight], 1)
    drk_ref[...] = (dk_acc[0:SET, :] * (w2 * SCALE)).astype(BF)
    drv_ref[...] = (dv_acc[0:SET, :] * w2).astype(BF)

    def finish_bwd(h, _):
        col = pl.ds(pl.multiple_of(h * HD, HD), HD)
        dq_ref[:, col] = (dq_acc[h].T * (weight * SCALE)).astype(BF)
        return 0

    lax.fori_loop(0, HEADS, finish_bwd, 0)

    mine = lax.broadcasted_iota(jnp.int32, (64, 256), 0) + (kv * 8 + grp) * 64 < plen
    for d in range(4):
        src = kvat(4 - d)
        cols = pl.ds(pl.multiple_of(src * 256, 256), 256)
        if d == 0:
            rows = pl.ds(pl.multiple_of(kv * 64, 64), 64)
            got_k, got_v = out_buf[0, 0, rows, :], out_buf[0, 1, rows, :]
        else:
            owners[d - 1].wait_recv()
            got_k, got_v = fin[d, 0], fin[d, 1]
        dpk_ref[:, cols] = jnp.where(mine, got_k.astype(F32) * (w2 * SCALE), 0.0)
        dpv_ref[:, cols] = jnp.where(mine, got_v.astype(F32) * w2, 0.0)

    for c in spread + gather + [w_x] + w_z + w_y + list(half.values()) + list(full.values()) + [sum_x] + owners:
        c.wait_send()


def on_device(
    queries, resp_keys, resp_values, prompt_keys, prompt_values, grad_out, resp_len, prompt_len
):
    vm = pl.BlockSpec(memory_space=pltpu.VMEM)
    sm = pl.BlockSpec(memory_space=pltpu.SMEM)
    shape = jax.ShapeDtypeStruct
    dma = pltpu.SemaphoreType.DMA
    outs = pl.pallas_call(
        kernel,
        out_shape=[
            shape((256, 2048), BF), shape((256, 2048), BF), shape((256, 256), BF), shape((256, 256), BF),
            shape((64, 1024), F32), shape((64, 1024), F32),
        ],
        in_specs=[sm, sm] + [vm] * 6,
        out_specs=[vm] * 6,
        scratch_shapes=[
            pltpu.VMEM((8, 2, SET, 256), BF),
            pltpu.VMEM((HEADS, 2304, SLOTS), BF),
            pltpu.VMEM((HEADS, HD + 16, SLOTS), F32),
            pltpu.VMEM((HEADS, HD, SLOTS), F32),
            pltpu.VMEM((5, HEADS, 1, SLOTS), F32),
            pltpu.VMEM((HEADS, 1, SLOTS), F32),
            pltpu.VMEM((2, 2304, 256), BF),
            pltpu.VMEM((2, 2304, 256), BF),
            pltpu.VMEM((2, HD, 2304), BF),
            pltpu.VMEM((2, HD + 16, 2304), BF),
            pltpu.VMEM((HEADS, SLOTS, 256), BF),
            pltpu.VMEM((HEADS, SLOTS, 256), BF),
            pltpu.VMEM((PC, SLOTS), F32),
            pltpu.VMEM((PC, SLOTS), F32),
            pltpu.VMEM((PC, 256), F32),
            pltpu.VMEM((PC, 256), F32),
            pltpu.VMEM((8, 2, SET, 256), BF),
            pltpu.VMEM((2, 2, 2, 128, 256), BF),
            pltpu.VMEM((2, 2, 2, SET, 256), BF),
            pltpu.VMEM((2, SET, 256), BF),
            pltpu.VMEM((4, 2, 64, 256), BF),
            pltpu.VMEM((3, 8, 128), F32),
            pltpu.VMEM((7, 8, 128), F32),
            dma((6,)), dma((6,)), dma((9,)), dma((9,)), dma((4,)), dma((4,)), dma((4,)), dma((4,)),
            dma(()), dma(()), dma((4,)), dma((4,)), dma((7,)), dma((7,)),
        ],
        compiler_params=pltpu.CompilerParams(
            collective_id=0, has_side_effects=True, vmem_limit_bytes=60 * 2**20
        ),
        name="attention",
    )(
        resp_len, prompt_len, queries.reshape(256, 2048), grad_out.reshape(256, 2048),
        resp_keys.reshape(256, 256), resp_values.reshape(256, 256),
        prompt_keys.reshape(64, 1024), prompt_values.reshape(64, 1024),
    )
    attended, grad_q, grad_rk, grad_rv, grad_pk, grad_pv = outs
    return (
        attended.reshape(queries.shape),
        grad_q.reshape(queries.shape),
        grad_rk.reshape(resp_keys.shape),
        grad_rv.reshape(resp_values.shape),
        grad_pk.reshape(1, 64, 1024),
        grad_pv.reshape(1, 64, 1024),
    )


def solution(mesh):
    wide = P("prompt", "grp", None, "kv")
    rows = P("prompt", ("kv", "grp"), None)
    return jax.shard_map(
        on_device,
        mesh=mesh,
        in_specs=(wide, wide, wide, rows, rows, wide, P("prompt", "grp"), P("prompt")),
        out_specs=(wide, wide, wide, wide, rows, rows),
        check_vma=False,
    )
```

time: 524 us -> 99.4 us (0.19)
  waiting for transfers between devices: 185 us -> 0 us
  blocking collectives: 115 us -> 0 us
  Pallas kernels: 0 us -> 90 us
  matrix products: 84.4 us -> 0 us
  local copies, waits for them, and re-layouts: 83.8 us -> 6.46 us
  other arithmetic: 23.8 us -> 0 us
  between operations: 15.9 us -> 1.95 us
  loops' own time: 8.3 us -> 0 us
  starting transfers between devices: 5.53 us -> 0 us
    unnamed x4 -> x0, waiting for transfers between devices: 97.8 us -> none
    pallas_call x0 -> x1, Pallas kernels: none -> 90 us  [on_device(): pl.pallas_call(kernel, out_shape=[shape((256, 2048), BF), shape((256, 204...]
    psum x1 -> x0, blocking collectives: 85.2 us -> none  [on_device(): lax.psum(jnp.sum(resp_len).astype(jnp.float32), ('grp', 'prompt'))]
    dot_general x34 -> x0, matrix products: 84.4 us -> none  [the longest x4 22 us: compute(): jnp.einsum('kgrj,jkd->rkgd', probs, value_block, preferred_element_type=j...]
    all_gather x2 -> x0, waiting for transfers between devices: 74.5 us -> none  [the longest x1 74.5 us: on_device(): lax.all_gather(prompt_values, ('kv', 'grp'), axis=1, tiled=True)]
    all_to_all x1 -> x0, blocking collectives: 29.4 us -> none  [on_device(): lax.all_to_all(partial_values, 'kv', split_axis=1, concat_axis=2, tiled=T...]
    dynamic_slice x26 -> x0, local copies, waits for them, and re-layouts: 24.1 us -> none  [the longest x24 19.6 us: on_device(): lax.scan(stat_step, (start_high, start_sum), (key_blocks, block_ids))]
    unnamed x29 -> x16, local copies, waits for them, and re-layouts: 25.4 us -> 6.46 us
  transfers between devices with their start and end apart: 4 -> 0, of which waited for: 3 -> 0; matrix products, arithmetic and copies ran while one was open for 9% -> 0% of each run, Pallas kernels for 0% -> 0%
where the time goes in v1:
time: 99.4 us; the launch traced here: 98.4 us
  Pallas kernels  90 us (91%)
  local copies, waits for them, and re-layouts  6.46 us (6%)
  between operations  1.95 us (2%)
    pallas_call x1, Pallas kernels, on_device(): pl.pallas_call(kernel, out_shape=[shape((256, 2048), BF), shape((256, 204...  90 us
    unnamed x16, local copies, waits for them, and re-layouts  6.46 us

profile of v1, /device:TPU:1, one launch (start us, length us, event | category | flops | bytes accessed | tf_op | source)
XLA Modules:
  0.0 98.4 jit_solution(5799325295013245516)
XLA Ops:
  1.9 90.0 %attention.1 = (bf16[256,2048]{1,0:T(8,128)(2,1)}, bf16[256,2048]{1,0:T(8,128)(2,1)}, bf16[256,256]{1,0:T(8,128)(2,1)}, bf16[256,256]{1,0:T(8,128)(2,1)}, f32[64,1024]{1,0:T(8,128)}, /*index=5*/f32[64,1024]{1,0:T(8,128)}) custom-call(s32[1,1]{1,0:T(1,128)S(6)} %copy.20.rl_ref, s32[1]{0:T(128)S(6)} %copy.21.pl_ref, bf16[256,2048]{1,0:T(8,128)(2,1)} %bitcast.12, ...), custom_call_target="tpu_custom_call" | custom-call | tf_op jit(solution)/shard_map/attention/pallas_call | solution.py:405
  92.0 0.0 copy-start
  92.0 2.4 %copy.22 = bf16[1,1,256,2048]{3,2,1,0:T(8,128)(2,1)} copy(bf16[1,1,256,2048]{3,2,1,0:T(8,128)(2,1)} %bitcast.15) | data formatting | bytes 2097152
  94.4 0.0 copy-done
  94.4 0.0 copy-start.4
  94.4 0.0 copy-start.3
  94.4 1.0 copy.23
  95.3 0.0 copy-done.4
  95.4 0.0 copy-start.2
  95.4 0.7 copy.24
  96.0 0.0 copy-done.3
  96.0 0.7 copy.25
  96.7 0.0 copy-done.2
  96.7 0.0 copy-start.1
  96.7 0.7 copy.26
  97.4 0.3 copy-done.1
  97.7 0.7 copy.27
Async XLA Ops:
  92.0 2.4 %copy-start = (bf16[256,2048]{1,0:T(8,128)(2,1)S(1)}, bf16[256,2048]{1,0:T(8,128)(2,1)}, u32[]{:S(2)}) copy-start(bf16[256,2048]{1,0:T(8,128)(2,1)} %get-tuple-element.13) | copy-start | bytes 3145732
  94.4 1.0 %copy-start.4 = (bf16[256,256]{1,0:T(8,128)(2,1)S(1)}, bf16[256,256]{1,0:T(8,128)(2,1)}, u32[]{:S(2)}) copy-start(bf16[256,256]{1,0:T(8,128)(2,1)} %get-tuple-element.14) | copy-start | bytes 393220
  94.4 1.7 %copy-start.3 = (bf16[256,256]{1,0:T(8,128)(2,1)S(1)}, bf16[256,256]{1,0:T(8,128)(2,1)}, u32[]{:S(2)}) copy-start(bf16[256,256]{1,0:T(8,128)(2,1)} %get-tuple-element.15) | copy-start | bytes 393220
  95.4 1.3 %copy-start.2 = (f32[64,1024]{1,0:T(8,128)S(1)}, f32[64,1024]{1,0:T(8,128)}, u32[]{:S(2)}) copy-start(f32[64,1024]{1,0:T(8,128)} %get-tuple-element.16) | copy-start | bytes 786436
  96.7 1.0 %copy-start.1 = (f32[64,1024]{1,0:T(8,128)S(1)}, f32[64,1024]{1,0:T(8,128)}, u32[]{:S(2)}) copy-start(f32[64,1024]{1,0:T(8,128)} %get-tuple-element.17) | copy-start | bytes 786436

commit v2 on v1

v2 whole, which is shorter than its diff:
```python
import functools

import jax
import jax.numpy as jnp
from jax import lax
from jax.experimental import pallas as pl
from jax.experimental.pallas import tpu as pltpu
from jax.sharding import PartitionSpec as P

F32 = jnp.float32
BF = jnp.bfloat16
MESH = pl.DeviceIdType.MESH
HD = 128
QPG = 8
SCALE = HD ** (-0.5)
LOG2E = 1.4426950408889634
NT = (((1,), (1,)), ((), ()))
NN = (((1,), (0,)), ((), ()))
SET = 256
PC = 512
HEADS = 16
SLOTS = 256
RESP_AT = 2048
SETS = ((0, 0), (0, 3), (0, 1), (1, 0), (1, 1), (1, 3), (0, 2), (1, 2))


def dot(a, b, dims):
    return lax.dot_general(a, b, dims, preferred_element_type=F32)


def cat(parts, axis):
    return parts[0] if len(parts) == 1 else jnp.concatenate(parts, axis)


def kernel(
    rl_ref, pl_ref, q_ref, do_ref, rk_ref, rv_ref, pk_ref, pv_ref,
    o_ref, dq_ref, drk_ref, drv_ref, dpk_ref, dpv_ref,
    sets, p_ref, o_acc, dq_acc, mc, lse, delta, k_n, k_t, v_t, q_t, d_t, s_buf, ds_buf, dc_buf,
    dk_acc, dv_acc, out_buf, own, half_in, full_in, x_in, fin, w_own, w_in,
    a2a_s, a2a_r, gs, gr, hs, hr, fs, fr, xs, xr, ks, kr, ws, wr,
):
    kv = lax.axis_index("kv")
    grp = lax.axis_index("grp")
    prm = lax.axis_index("prompt")
    xh = grp // 4
    z = grp % 4
    zat = lambda d: {"grp": xh * 4 + (z + d) % 4}
    zp, zm, xp = zat(1), zat(3), {"grp": (1 - xh) * 4 + z}
    kvat = lambda d: (kv + d) % 4
    yat = lambda d: {"prompt": (prm + d) % 4}

    peers = [{"kv": kvat(d)} for d in (1, 2, 3)] + [zat(d) for d in (1, 2, 3)]
    peers += [yat(d) for d in (1, 2, 3)] + [xp]
    barrier = pltpu.get_barrier_semaphore()
    for peer in peers:
        pl.semaphore_signal(barrier, inc=1, device_id=peer, device_id_type=MESH)
    pl.semaphore_wait(barrier, len(peers))

    def cp(src, dst, ssem, rsem, dev):
        return pltpu.make_async_remote_copy(
            src_ref=src, dst_ref=dst, send_sem=ssem, recv_sem=rsem, device_id=dev, device_id_type=MESH
        )

    spread = []
    for d in (1, 2, 3):
        cols = pl.ds(pl.multiple_of(kvat(d) * 256, 256), 256)
        rows = pl.ds(pl.multiple_of(kv * 64, 64), 64)
        for t, ref in ((0, pk_ref), (1, pv_ref)):
            i = (d - 1) * 2 + t
            spread.append(cp(ref.at[:, cols], sets.at[0, t, rows, :], a2a_s.at[i], a2a_r.at[i], {"kv": kvat(d)}))
    lo, hi = pl.ds(0, 128), pl.ds(128, 128)
    to_x = cp(sets.at[0], sets.at[3], gs.at[0], gr.at[0], xp)
    to_p = cp(sets.at[0], sets.at[1], gs.at[1], gr.at[1], zp)
    to_m = cp(sets.at[0], sets.at[2], gs.at[2], gr.at[2], zm)
    on_p = cp(sets.at[1, :, lo], sets.at[6, :, lo], gs.at[3], gr.at[3], zp)
    on_m = cp(sets.at[2, :, hi], sets.at[6, :, hi], gs.at[4], gr.at[4], zm)
    xto_p = cp(sets.at[3], sets.at[5], gs.at[5], gr.at[5], zp)
    xto_m = cp(sets.at[3], sets.at[4], gs.at[6], gr.at[6], zm)
    xon_p = cp(sets.at[5, :, lo], sets.at[7, :, lo], gs.at[7], gr.at[7], zp)
    xon_m = cp(sets.at[4, :, hi], sets.at[7, :, hi], gs.at[8], gr.at[8], zm)
    gather = [to_x, to_p, to_m, on_p, on_m, xto_p, xto_m, xon_p, xon_m]
    w_x = cp(w_own.at[0], w_in.at[0], ws.at[0], wr.at[0], xp)
    w_z = [cp(w_own.at[1], w_in.at[d], ws.at[d], wr.at[d], zat(d)) for d in (1, 2, 3)]
    w_y = [cp(w_own.at[2], w_in.at[3 + d], ws.at[3 + d], wr.at[3 + d], yat(d)) for d in (1, 2, 3)]
    half = {}
    full = {}
    for dx, s in ((0, 6), (1, 7)):
        half[dx, 0] = cp(out_buf.at[s, :, :, lo], half_in.at[dx, 0], hs.at[dx * 2], hr.at[dx * 2], zp)
        half[dx, 1] = cp(out_buf.at[s, :, :, hi], half_in.at[dx, 1], hs.at[dx * 2 + 1], hr.at[dx * 2 + 1], zm)
    for dx, d, s in ((0, 0, 2), (0, 1, 1), (1, 0, 4), (1, 1, 5)):
        i = dx * 2 + d
        full[dx, d] = cp(out_buf.at[s], full_in.at[dx, d], fs.at[i], fr.at[i], zm if d else zp)
    sum_x = cp(out_buf.at[3], x_in, xs, xr, xp)
    owners = []
    for d in (1, 2, 3):
        rows = pl.ds(pl.multiple_of(kvat(d) * 64, 64), 64)
        owners.append(cp(own.at[:, rows, :], fin.at[d], ks.at[d], kr.at[d], {"kv": kvat(d)}))

    for c in spread:
        c.start()
    w_own[0] = jnp.full((8, 128), rl_ref[0, 0].astype(F32))
    w_x.start()

    rows = pl.ds(pl.multiple_of(kv * 64, 64), 64)
    cols = pl.ds(pl.multiple_of(kv * 256, 256), 256)
    sets[0, 0, rows, :] = pk_ref[:, cols]
    sets[0, 1, rows, :] = pv_ref[:, cols]

    live = jnp.where(lax.broadcasted_iota(jnp.int32, (HD, SLOTS), 1) < rl_ref[0, 0], 1.0, 0.0).astype(BF)

    def stage_queries(i, _):
        for u in range(4):
            h = i * 4 + u
            col = pl.ds(pl.multiple_of(h * HD, HD), HD)
            q_t[h] = q_ref[:, col].T
            d_t[h] = do_ref[:, col].T * live
            dq_acc[h] = jnp.zeros((HD, SLOTS), F32)
        return 0

    lax.fori_loop(0, HEADS // 4, stage_queries, 0)
    for kh in range(2):
        head = slice(kh * HD, (kh + 1) * HD)
        k_t[kh, :, RESP_AT:] = rk_ref[:, head].T
        v_t[kh, 0:HD, RESP_AT:] = rv_ref[:, head].T
        v_t[kh, HD:, RESP_AT:] = jnp.ones((16, SET), BF)

    plen = pl_ref[0]

    def valid_keys(s, shape, axis):
        dx, dz = SETS[s]
        owner = (xh if dx == 0 else 1 - xh) * 4 + (z + dz) % 4
        r = lax.broadcasted_iota(jnp.int32, shape, axis)
        index = ((r // 64) * 8 + owner) * 64 + r % 64
        return jnp.where(index < plen, 1.0, 0.0).astype(BF)

    def put_set(s):
        by_row = valid_keys(s, (SET, HD), 0)
        by_col = valid_keys(s, (HD, SET), 1)
        at = slice(s * SET, (s + 1) * SET)
        for kh in range(2):
            head = slice(kh * HD, (kh + 1) * HD)
            k = sets[s, 0, :, head]
            k_n[at, head] = k * by_row + k[0:1, :] * (1 - by_row)
            k_t[kh, :, at] = k.T * by_col
            v_t[kh, 0:HD, at] = sets[s, 1, :, head].T * by_col
            v_t[kh, HD:, at] = by_col[0:16, :]

    def scores(j, h, rows, keys, mask, s_ref):
        top = None
        for r in range(0, rows, 256):
            s = dot(keys(r, h // QPG), q_t[h], NN) * (SCALE * LOG2E)
            if mask is not None:
                s = jnp.where(mask, s, -1e30)
            s_ref[r:r + 256, :] = s
            b = jnp.max(s.reshape(32, 8, SLOTS), 0)
            top = b if top is None else jnp.maximum(top, b)
        m = jnp.max(top, 0, keepdims=True)
        mc[j, h] = m if mask is not None else jnp.maximum(mc[j - 1, h], m)

    def attend(j, h, rows, at, s_ref, first):
        m = mc[j, h]
        parts = []
        for r in range(0, rows, 256):
            p = jnp.exp2(s_ref[r:r + 256, :] - m).astype(BF)
            p_ref[h, pl.ds(at + r, 256), :] = p
            parts.append(p)
        new = dot(v_t[h // QPG, :, pl.ds(at, rows)], cat(parts, 0), NN)
        o_acc[h] = new if first else o_acc[h] * jnp.exp2(mc[j - 1, h] - m) + new

    def forward(j, rows, at, keys, mask):
        first = mask is not None
        for h in range(HEADS + 1):
            if h < HEADS:
                scores(j, h, rows, keys, mask, s_buf.at[h % 2])
            if h > 0:
                attend(j, h - 1, rows, at, s_buf.at[(h - 1) % 2], first)

    for c in spread:
        c.wait_recv()
    for c in (to_x, to_p, to_m):
        c.start()
    t = lax.broadcasted_iota(jnp.int32, (SET, SLOTS), 0)
    i = lax.broadcasted_iota(jnp.int32, (SET, SLOTS), 1)
    forward(0, SET, RESP_AT, lambda r, kh: rk_ref[:, kh * HD:(kh + 1) * HD], (t <= i) & (t < rl_ref[0, 0]))
    w_x.wait_recv()
    w_own[1] = w_own[0] + w_in[0]
    for c in w_z:
        c.start()
    put_set(0)

    def fwd_chunk(c, _):
        @pl.when(c == 0)
        def _():
            to_p.wait_recv()
            on_p.start()
            to_m.wait_recv()
            on_m.start()
            put_set(1)

        @pl.when(c == 1)
        def _():
            to_x.wait_recv()
            xto_p.start()
            xto_m.start()
            put_set(2)
            put_set(3)
            for w in w_z:
                w.wait_recv()
            w_own[2] = w_own[1] + (w_in[1] + w_in[2] + w_in[3])
            for w in w_y:
                w.start()

        @pl.when(c == 2)
        def _():
            xto_p.wait_recv()
            xon_p.start()
            xto_m.wait_recv()
            xon_m.start()
            put_set(4)
            put_set(5)

        @pl.when(c == 3)
        def _():
            on_p.wait_recv()
            on_m.wait_recv()
            put_set(6)
            xon_p.wait_recv()
            xon_m.wait_recv()
            put_set(7)

        at = pl.multiple_of(c * PC, PC)
        forward(c + 1, PC, at, lambda r, kh: k_n[pl.ds(at + r, 256), kh * HD:(kh + 1) * HD], None)
        return 0

    lax.fori_loop(0, 4, fwd_chunk, 0)

    def finish_fwd(i, _):
        for u in range(4):
            h = i * 4 + u
            col = pl.ds(pl.multiple_of(h * HD, HD), HD)
            o = o_acc[h]
            total = o[HD:HD + 1, :]
            out = (o[0:HD, :] * (1.0 / total)).astype(BF)
            o_ref[:, col] = out.T
            delta[h] = jnp.sum(out.astype(F32) * d_t[h].astype(F32), 0, keepdims=True)
            lse[h] = mc[4, h] + jnp.log2(total)
        return 0

    lax.fori_loop(0, HEADS // 4, finish_fwd, 0)
    for w in w_y:
        w.wait_recv()
    count = w_own[2] + (w_in[4] + w_in[5] + w_in[6])
    weight = (8192.0 / count)[0:1, :]

    def weigh(j, h, rows, at, values, ds_ref, dc_ref):
        corr = jnp.exp2(mc[j, h] - lse[h])
        dc = (d_t[h].astype(F32) * corr).astype(BF)
        dc_ref[...] = dc
        cd = corr * delta[h]
        for r in range(0, rows, 256):
            dp = dot(values(r, h // QPG), dc, NN) - cd
            ds_ref[r:r + 256, :] = p_ref[h, pl.ds(at + r, 256), :] * dp.astype(BF)

    def spread_back(h, rows, at, ds_ref, dc_ref):
        kh = h // QPG
        dq_acc[h] += dot(k_t[kh, :, pl.ds(at, rows)], ds_ref[0:rows, :], NN)
        for r in range(0, rows, 256):
            dv = dot(dc_ref[...], p_ref[h, pl.ds(at + r, 256), :], NT)
            dk = dot(q_t[h], ds_ref[r:r + 256, :], NT)
            if h % QPG == 0:
                dv_acc[kh, :, r:r + 256] = dv
                dk_acc[kh, :, r:r + 256] = dk
            else:
                dv_acc[kh, :, r:r + 256] += dv
                dk_acc[kh, :, r:r + 256] += dk

    def backward(j, rows, at, values):
        for h in range(HEADS + 1):
            if h < HEADS:
                weigh(j, h, rows, at, values, ds_buf.at[h % 2], dc_buf.at[h % 2])
            if h > 0:
                spread_back(h - 1, rows, at, ds_buf.at[(h - 1) % 2], dc_buf.at[(h - 1) % 2])

    def acc_of(s):
        r = slice((s % 2) * SET, (s % 2 + 1) * SET)
        return [cat([a[0, :, r], a[1, :, r]], 0) for a in (dk_acc, dv_acc)]

    def bwd_chunk(i, _):
        c = 3 - i
        at = pl.multiple_of(c * PC, PC)
        backward(c + 1, PC, at, lambda r, kh: sets[2 * c + r // SET, 1, :, kh * HD:(kh + 1) * HD])

        @pl.when(c == 3)
        def _():
            for dx, s in ((1, 7), (0, 6)):
                for t, a in enumerate(acc_of(s)):
                    out_buf[s, t] = a.astype(BF)
                half[dx, 0].start()
                half[dx, 1].start()

        @pl.when(c == 2)
        def _():
            for d, s in ((0, 4), (1, 5)):
                half[1, d].wait_recv()
                for t, a in enumerate(acc_of(s)):
                    put_half(s, t, d, a, half_in[1, d, t])
                full[1, d].start()

        @pl.when(c == 1)
        def _():
            half[0, 0].wait_recv()
            for t, a in enumerate(acc_of(2)):
                put_half(2, t, 0, a, half_in[0, 0, t])
            full[0, 0].start()
            full[1, 0].wait_recv()
            full[1, 1].wait_recv()
            for t, a in enumerate(acc_of(3)):
                out_buf[3, t] = (a + full_in[1, 0, t].astype(F32) + full_in[1, 1, t].astype(F32)).astype(BF)
            sum_x.start()

        @pl.when(c == 0)
        def _():
            half[0, 1].wait_recv()
            for t, a in enumerate(acc_of(1)):
                put_half(1, t, 1, a, half_in[0, 1, t])
            full[0, 1].start()
            full[0, 0].wait_recv()
            full[0, 1].wait_recv()
            sum_x.wait_recv()
            for t, a in enumerate(acc_of(0)):
                more = full_in[0, 0, t].astype(F32) + full_in[0, 1, t].astype(F32) + x_in[t].astype(F32)
                own[t] = (a + more).astype(BF).T
            for o in owners:
                o.start()

        return 0

    def put_half(s, t, d, a, part):
        near, far = slice(d * 128, d * 128 + 128), slice(128 - d * 128, 256 - d * 128)
        out_buf[s, t, :, near] = (a[:, near] + part.astype(F32)).astype(BF)
        out_buf[s, t, :, far] = a[:, far].astype(BF)

    lax.fori_loop(0, 4, bwd_chunk, 0)
    backward(0, SET, RESP_AT, lambda r, kh: rv_ref[:, kh * HD:(kh + 1) * HD])
    w2 = cat([weight, weight], 1)
    acc_k, acc_v = acc_of(0)
    drk_ref[...] = (acc_k * (w2 * SCALE)).T.astype(BF)
    drv_ref[...] = (acc_v * w2).T.astype(BF)

    def finish_bwd(i, _):
        for u in range(4):
            h = i * 4 + u
            col = pl.ds(pl.multiple_of(h * HD, HD), HD)
            dq_ref[:, col] = (dq_acc[h] * (w2 * SCALE)).astype(BF).T
        return 0

    lax.fori_loop(0, HEADS // 4, finish_bwd, 0)

    mine = lax.broadcasted_iota(jnp.int32, (64, 256), 0) + (kv * 8 + grp) * 64 < plen
    for d in range(4):
        src = kvat(4 - d)
        cols = pl.ds(pl.multiple_of(src * 256, 256), 256)
        if d == 0:
            rows = pl.ds(pl.multiple_of(kv * 64, 64), 64)
            got_k, got_v = own[0, rows, :], own[1, rows, :]
        else:
            owners[d - 1].wait_recv()
            got_k, got_v = fin[d, 0], fin[d, 1]
        dpk_ref[:, cols] = jnp.where(mine, got_k.astype(F32) * (w2 * SCALE), 0.0)
        dpv_ref[:, cols] = jnp.where(mine, got_v.astype(F32) * w2, 0.0)

    for c in spread + gather + [w_x] + w_z + w_y + list(half.values()) + list(full.values()) + [sum_x] + owners:
        c.wait_send()


def on_device(
    queries, resp_keys, resp_values, prompt_keys, prompt_values, grad_out, resp_len, prompt_len
):
    vm = pl.BlockSpec(memory_space=pltpu.VMEM)
    sm = pl.BlockSpec(memory_space=pltpu.SMEM)
    shape = jax.ShapeDtypeStruct
    dma = pltpu.SemaphoreType.DMA
    outs = pl.pallas_call(
        kernel,
        out_shape=[
            shape((256, 2048), BF), shape((256, 2048), BF), shape((256, 256), BF), shape((256, 256), BF),
            shape((64, 1024), F32), shape((64, 1024), F32),
        ],
        in_specs=[sm, sm] + [vm] * 6,
        out_specs=[vm] * 6,
        scratch_shapes=[
            pltpu.VMEM((8, 2, SET, 256), BF),
            pltpu.VMEM((HEADS, 2304, SLOTS), BF),
            pltpu.VMEM((HEADS, HD + 16, SLOTS), F32),
            pltpu.VMEM((HEADS, HD, SLOTS), F32),
            pltpu.VMEM((5, HEADS, 1, SLOTS), F32),
            pltpu.VMEM((HEADS, 1, SLOTS), F32),
            pltpu.VMEM((HEADS, 1, SLOTS), F32),
            pltpu.VMEM((RESP_AT, 256), BF),
            pltpu.VMEM((2, HD, 2304), BF),
            pltpu.VMEM((2, HD + 16, 2304), BF),
            pltpu.VMEM((HEADS, HD, SLOTS), BF),
            pltpu.VMEM((HEADS, HD, SLOTS), BF),
            pltpu.VMEM((2, PC, SLOTS), F32),
            pltpu.VMEM((2, PC, SLOTS), BF),
            pltpu.VMEM((2, HD, SLOTS), BF),
            pltpu.VMEM((2, HD, PC), F32),
            pltpu.VMEM((2, HD, PC), F32),
            pltpu.VMEM((8, 2, 256, SET), BF),
            pltpu.VMEM((2, SET, 256), BF),
            pltpu.VMEM((2, 2, 2, 256, 128), BF),
            pltpu.VMEM((2, 2, 2, 256, SET), BF),
            pltpu.VMEM((2, 256, SET), BF),
            pltpu.VMEM((4, 2, 64, 256), BF),
            pltpu.VMEM((3, 8, 128), F32),
            pltpu.VMEM((7, 8, 128), F32),
            dma((6,)), dma((6,)), dma((9,)), dma((9,)), dma((4,)), dma((4,)), dma((4,)), dma((4,)),
            dma(()), dma(()), dma((4,)), dma((4,)), dma((7,)), dma((7,)),
        ],
        compiler_params=pltpu.CompilerParams(
            collective_id=0, has_side_effects=True, vmem_limit_bytes=60 * 2**20
        ),
        name="attention",
    )(
        resp_len, prompt_len, queries.reshape(256, 2048), grad_out.reshape(256, 2048),
        resp_keys.reshape(256, 256), resp_values.reshape(256, 256),
        prompt_keys.reshape(64, 1024), prompt_values.reshape(64, 1024),
    )
    attended, grad_q, grad_rk, grad_rv, grad_pk, grad_pv = outs
    return (
        attended.reshape(queries.shape),
        grad_q.reshape(queries.shape),
        grad_rk.reshape(resp_keys.shape),
        grad_rv.reshape(resp_values.shape),
        grad_pk.reshape(1, 64, 1024),
        grad_pv.reshape(1, 64, 1024),
    )


def solution(mesh):
    wide = P("prompt", "grp", None, "kv")
    rows = P("prompt", ("kv", "grp"), None)
    return jax.shard_map(
        on_device,
        mesh=mesh,
        in_specs=(wide, wide, wide, rows, rows, wide, P("prompt", "grp"), P("prompt")),
        out_specs=(wide, wide, wide, wide, rows, rows),
        check_vma=False,
    )
```

time: 99.4 us -> 81.8 us (0.82)
  Pallas kernels: 90 us -> 73.1 us
    pallas_call x1, Pallas kernels: 90 us -> 73.1 us  [on_device(): pl.pallas_call(kernel, out_shape=[shape((256, 2048), BF), shape((256, 204...]
where the time goes in v2:
time: 81.8 us; the launch traced here: 81.5 us
  Pallas kernels  73.1 us (89%)
  local copies, waits for them, and re-layouts  6.46 us (8%)
  between operations  1.95 us (2%)
    pallas_call x1, Pallas kernels, on_device(): pl.pallas_call(kernel, out_shape=[shape((256, 2048), BF), shape((256, 204...  73.1 us
    unnamed x16, local copies, waits for them, and re-layouts  6.46 us

profile of v2, /device:TPU:1, one launch (start us, length us, event | category | flops | bytes accessed | tf_op | source)
XLA Modules:
  0.0 81.5 jit_solution(17242067825875970206)
XLA Ops:
  1.9 73.1 %attention.1 = (bf16[256,2048]{1,0:T(8,128)(2,1)}, bf16[256,2048]{1,0:T(8,128)(2,1)}, bf16[256,256]{1,0:T(8,128)(2,1)}, bf16[256,256]{1,0:T(8,128)(2,1)}, f32[64,1024]{1,0:T(8,128)}, /*index=5*/f32[64,1024]{1,0:T(8,128)}) custom-call(s32[1,1]{1,0:T(1,128)S(6)} %copy.20.rl_ref, s32[1]{0:T(128)S(6)} %copy.21.pl_ref, bf16[256,2048]{1,0:T(8,128)(2,1)} %bitcast.12, ...), custom_call_target="tpu_custom_call" | custom-call | tf_op jit(solution)/shard_map/attention/pallas_call | solution.py:383
  75.0 0.0 copy-start
  75.0 2.4 %copy.22 = bf16[1,1,256,2048]{3,2,1,0:T(8,128)(2,1)} copy(bf16[1,1,256,2048]{3,2,1,0:T(8,128)(2,1)} %bitcast.15) | data formatting | bytes 2097152
  77.4 0.0 copy-done
  77.4 0.0 copy-start.4
  77.4 0.0 copy-start.3
  77.4 1.0 %copy.23 = bf16[1,1,256,2048]{3,2,1,0:T(8,128)(2,1)} copy(bf16[1,1,256,2048]{3,2,1,0:T(8,128)(2,1)S(1)} %bitcast.14) | data formatting | bytes 2097152
  78.4 0.0 copy-done.4
  78.4 0.0 copy-start.2
  78.4 0.7 copy.24
  79.1 0.0 copy-done.3
  79.1 0.7 copy.25
  79.7 0.0 copy-done.2
  79.7 0.0 copy-start.1
  79.7 0.7 copy.26
  80.4 0.3 copy-done.1
  80.8 0.7 copy.27
Async XLA Ops:
  75.0 2.4 %copy-start = (bf16[256,2048]{1,0:T(8,128)(2,1)S(1)}, bf16[256,2048]{1,0:T(8,128)(2,1)}, u32[]{:S(2)}) copy-start(bf16[256,2048]{1,0:T(8,128)(2,1)} %get-tuple-element.13) | copy-start | bytes 3145732
  77.4 1.0 %copy-start.4 = (bf16[256,256]{1,0:T(8,128)(2,1)S(1)}, bf16[256,256]{1,0:T(8,128)(2,1)}, u32[]{:S(2)}) copy-start(bf16[256,256]{1,0:T(8,128)(2,1)} %get-tuple-element.14) | copy-start | bytes 393220
  77.4 1.7 %copy-start.3 = (bf16[256,256]{1,0:T(8,128)(2,1)S(1)}, bf16[256,256]{1,0:T(8,128)(2,1)}, u32[]{:S(2)}) copy-start(bf16[256,256]{1,0:T(8,128)(2,1)} %get-tuple-element.15) | copy-start | bytes 393220
  78.4 1.3 %copy-start.2 = (f32[64,1024]{1,0:T(8,128)S(1)}, f32[64,1024]{1,0:T(8,128)}, u32[]{:S(2)}) copy-start(f32[64,1024]{1,0:T(8,128)} %get-tuple-element.16) | copy-start | bytes 786436
  79.7 1.0 %copy-start.1 = (f32[64,1024]{1,0:T(8,128)S(1)}, f32[64,1024]{1,0:T(8,128)}, u32[]{:S(2)}) copy-start(f32[64,1024]{1,0:T(8,128)} %get-tuple-element.17) | copy-start | bytes 786436

commit v3 on v2

v3 whole, which is shorter than its diff:
```python
import jax
import jax.numpy as jnp
from jax import lax
from jax.experimental import pallas as pl
from jax.experimental.pallas import tpu as pltpu
from jax.sharding import PartitionSpec as P

F32 = jnp.float32
BF = jnp.bfloat16
MESH = pl.DeviceIdType.MESH
HD = 128
QPG = 8
SCALE = HD ** (-0.5)
LOG2E = 1.4426950408889634
NT = (((1,), (1,)), ((), ()))
NN = (((1,), (0,)), ((), ()))
SET = 256
PC = 512
HEADS = 16
SLOTS = 256
RESP_AT = 2048
KEYS = 2304
SETS = ((0, 0), (0, 3), (0, 1), (1, 0), (1, 1), (1, 3), (0, 2), (1, 2))


def dot(a, b, dims):
    return lax.dot_general(a, b, dims, preferred_element_type=F32)


def cat(parts, axis):
    return parts[0] if len(parts) == 1 else jnp.concatenate(parts, axis)


def kernel(
    rl_ref, pl_ref, q_hbm, do_hbm, rk_hbm, rv_hbm, pk_hbm, pv_hbm,
    o_hbm, dq_hbm, drk_ref, drv_ref, dpk_ref, dpv_ref,
    sets, p_ref, ds_ref, o_acc, o_out, mc, lse, delta, k_n, k_t, v_t, r_kv, q_t, d_t,
    s_a, s_b, ds_a, ds_b, dc_a, dc_b, dk_acc, dv_acc,
    out_buf, own, half_in, plane_in, z_in, x_in, far_in, fin, w_own, w_in,
    ls, a2a_s, a2a_r, gs, gr, hs, hr, ks, kr, ws, wr,
):
    kv = lax.axis_index("kv")
    grp = lax.axis_index("grp")
    prm = lax.axis_index("prompt")
    xh = grp // 4
    z = grp % 4
    zat = lambda d: {"grp": xh * 4 + (z + d) % 4}
    zp, zm, xp = zat(1), zat(3), {"grp": (1 - xh) * 4 + z}
    kvat = lambda d: (kv + d) % 4
    yat = lambda d: {"prompt": (prm + d) % 4}
    my_rows = pl.ds(pl.multiple_of(kv * 64, 64), 64)
    head_cols = lambda who, t: pl.ds(pl.multiple_of(who * 256 + t * HD, HD), HD)

    pair = lambda i: pl.ds(i * 256, 256)
    local = []
    for i in range(8):
        local.append(pltpu.make_async_copy(q_hbm.at[:, pair(i)], ds_ref.at[i, 0:256, :], ls.at[i]))
        local.append(pltpu.make_async_copy(do_hbm.at[:, pair(i)], ds_ref.at[i, 256:512, :], ls.at[8 + i]))
    local.append(pltpu.make_async_copy(rk_hbm, r_kv.at[0], ls.at[16]))
    local.append(pltpu.make_async_copy(rv_hbm, r_kv.at[1], ls.at[17]))
    for t in range(2):
        for i, ref in ((0, pk_hbm), (1, pv_hbm)):
            local.append(
                pltpu.make_async_copy(
                    ref.at[:, head_cols(kv, t)], sets.at[t, 0, i, my_rows, :], ls.at[18 + t * 2 + i]
                )
            )
    for c in local:
        c.start()

    peers = [{"kv": kvat(d)} for d in (1, 2, 3)] + [zat(d) for d in (1, 2, 3)]
    peers += [yat(d) for d in (1, 2, 3)] + [xp]
    barrier = pltpu.get_barrier_semaphore()
    for peer in peers:
        pl.semaphore_signal(barrier, inc=1, device_id=peer, device_id_type=MESH)
    pl.semaphore_wait(barrier, len(peers))

    def cp(src, dst, ssem, rsem, dev):
        return pltpu.make_async_remote_copy(
            src_ref=src, dst_ref=dst, send_sem=ssem, recv_sem=rsem, device_id=dev, device_id_type=MESH
        )

    def spread(t):
        made = []
        for d in (1, 2, 3):
            for i, ref in ((0, pk_hbm), (1, pv_hbm)):
                n = (d - 1) * 2 + i
                made.append(
                    cp(ref.at[:, head_cols(kvat(d), t)], sets.at[t, 0, i, my_rows, :],
                       a2a_s.at[t, n], a2a_r.at[t, n], {"kv": kvat(d)})
                )
        return made

    lo, hi = pl.ds(0, 128), pl.ds(128, 128)

    def moved(t, n, src, dst, dev, rows=None):
        a, b = sets.at[t, src], sets.at[t, dst]
        if rows is not None:
            a, b = a.at[:, rows], b.at[:, rows]
        return cp(a, b, gs.at[t, n], gr.at[t, n], dev)

    to_x = lambda t: moved(t, 0, 0, 3, xp)
    to_p = lambda t: moved(t, 1, 0, 1, zp)
    to_m = lambda t: moved(t, 2, 0, 2, zm)
    on_p = lambda t: moved(t, 3, 1, 6, zp, lo)
    on_m = lambda t: moved(t, 4, 2, 6, zm, hi)
    xto_p = lambda t: moved(t, 5, 3, 5, zp)
    xto_m = lambda t: moved(t, 6, 3, 4, zm)
    far = lambda t: moved(t, 7, 6, 7, xp)
    gather = [to_x, to_p, to_m, on_p, on_m, xto_p, xto_m, far]
    w_x = cp(w_own.at[0], w_in.at[0], ws.at[0], wr.at[0], xp)
    w_z = [cp(w_own.at[1], w_in.at[d], ws.at[d], wr.at[d], zat(d)) for d in (1, 2, 3)]
    w_y = [cp(w_own.at[2], w_in.at[3 + d], ws.at[3 + d], wr.at[3 + d], yat(d)) for d in (1, 2, 3)]
    def summed(t, n, src, dst, dev):
        return cp(src, dst, hs.at[t, n], hr.at[t, n], dev)

    far_sum = lambda t: summed(t, 0, out_buf.at[t, 7], far_in.at[t], xp)
    half_p = lambda t: summed(t, 1, out_buf.at[t, 6, :, :, lo], half_in.at[t, 0], zp)
    half_m = lambda t: summed(t, 2, out_buf.at[t, 6, :, :, hi], half_in.at[t, 1], zm)
    plane_p = lambda t: summed(t, 3, out_buf.at[t, 4], plane_in.at[t, 0], zp)
    plane_m = lambda t: summed(t, 4, out_buf.at[t, 5], plane_in.at[t, 1], zm)
    z_p = lambda t: summed(t, 5, out_buf.at[t, 2], z_in.at[t, 0], zp)
    z_m = lambda t: summed(t, 6, out_buf.at[t, 1], z_in.at[t, 1], zm)
    x_sum = lambda t: summed(t, 7, out_buf.at[t, 3], x_in.at[t], xp)
    sums = [far_sum, half_p, half_m, plane_p, plane_m, z_p, z_m, x_sum]

    def to_owner(t, d):
        rows = pl.ds(pl.multiple_of(kvat(d) * 64, 64), 64)
        return cp(own.at[t, :, rows, :], fin.at[t, d], ks.at[t, d], kr.at[t, d], {"kv": kvat(d)})

    for t in range(2):
        for c in spread(t):
            c.start()
    w_own[0] = jnp.full((8, 128), rl_ref[0, 0].astype(F32))
    w_x.start()
    for c in local:
        c.wait()

    live = jnp.where(lax.broadcasted_iota(jnp.int32, (HD, SLOTS), 1) < rl_ref[0, 0], 1.0, 0.0).astype(BF)

    def stage_queries(i, _):
        for u in range(2):
            for v in range(2):
                h = i * 4 + u * 2 + v
                half = slice(v * HD, (v + 1) * HD)
                q_t[h] = ds_ref[i * 2 + u, 0:256, half].T
                d_t[h] = ds_ref[i * 2 + u, 256:512, half].T * live
        return 0

    lax.fori_loop(0, HEADS // 4, stage_queries, 0)
    for t in range(2):
        head = slice(t * HD, (t + 1) * HD)
        k_t[t, :, RESP_AT:] = r_kv[0, :, head].T
        v_t[t, 0:HD, RESP_AT:] = r_kv[1, :, head].T
        v_t[t, HD:, RESP_AT:] = jnp.ones((16, SET), BF)

    plen = pl_ref[0]

    def valid_keys(s, shape, axis):
        dx, dz = SETS[s]
        owner = (xh if dx == 0 else 1 - xh) * 4 + (z + dz) % 4
        r = lax.broadcasted_iota(jnp.int32, shape, axis)
        return jnp.where((r // 64) * 512 + r % 64 < plen - owner * 64, 1.0, 0.0).astype(BF)

    def put_set(t, s):
        by_row = valid_keys(s, (SET, HD), 0)
        by_col = valid_keys(s, (16, SET), 1)
        at = slice(s * SET, (s + 1) * SET)
        k = sets[t, s, 0]
        k_n[t, at, :] = k * by_row + k[0:1, :] * (1 - by_row)
        k_t[t, :, at] = k.T * by_col[0:1, :]
        v_t[t, 0:HD, at] = sets[t, s, 1].T * by_col[0:1, :]
        v_t[t, HD:, at] = by_col

    s_bufs, ds_bufs, dc_bufs = (s_a, s_b), (ds_a, ds_b), (dc_a, dc_b)

    def scores(t, j, u, rows, keys, mask):
        h = t * QPG + u
        s_ref = s_bufs[u % 2]
        top = None
        for r in range(0, rows, 256):
            s = dot(keys(r), q_t[h], NN) * (SCALE * LOG2E)
            if mask is not None:
                s = jnp.where(mask, s, -1e30)
            s_ref[r:r + 256, :] = s
            b = jnp.max(s.reshape(32, 8, SLOTS), 0)
            top = b if top is None else jnp.maximum(top, b)
        m = jnp.max(top, 0, keepdims=True)
        mc[j, h] = m if mask is not None else jnp.maximum(mc[j - 1, h], m)

    def attend(t, j, u, rows, at, first):
        h = t * QPG + u
        s_ref = s_bufs[u % 2]
        m = mc[j, h]
        parts = []
        for r in range(0, rows, 256):
            p = jnp.exp2(s_ref[r:r + 256, :] - m).astype(BF)
            p_ref[h, pl.ds(at + r, 256), :] = p
            parts.append(p)
        new = dot(v_t[t, :, pl.ds(at, rows)], cat(parts, 0), NN)
        o_acc[h] = new if first else o_acc[h] * jnp.exp2(mc[j - 1, h] - m) + new

    def forward(t, j, rows, at, keys, mask):
        for u in range(QPG + 1):
            if u < QPG:
                scores(t, j, u, rows, keys, mask)
            if u > 0:
                attend(t, j, u - 1, rows, at, mask is not None)

    def weigh(t, j, u, rows, at, values):
        h = t * QPG + u
        corr = jnp.exp2(mc[j, h] - lse[h])
        dc = (d_t[h].astype(F32) * corr).astype(BF)
        dc_bufs[u % 2][...] = dc
        cd = corr * delta[h]
        for r in range(0, rows, 256):
            dp = dot(values(r), dc, NN) - cd
            ds = p_ref[h, pl.ds(at + r, 256), :] * dp.astype(BF)
            ds_bufs[u % 2][r:r + 256, :] = ds
            ds_ref[h, pl.ds(at + r, 256), :] = ds

    def key_sums(t, u, rows, at):
        h = t * QPG + u
        for r in range(0, rows, 256):
            dv = dot(dc_bufs[u % 2][...], p_ref[h, pl.ds(at + r, 256), :], NT)
            dk = dot(q_t[h], ds_bufs[u % 2][r:r + 256, :], NT)
            if u == 0:
                dv_acc[:, r:r + 256] = dv
                dk_acc[:, r:r + 256] = dk
            else:
                dv_acc[:, r:r + 256] += dv
                dk_acc[:, r:r + 256] += dk

    def backward(t, j, rows, at, values):
        for u in range(QPG + 1):
            if u < QPG:
                weigh(t, j, u, rows, at, values)
            if u > 0:
                key_sums(t, u - 1, rows, at)

    def query_sums(t):
        for u in range(QPG):
            h = t * QPG + u
            dq = dot(k_t[t], ds_ref[h], NN) * (w2 * SCALE)
            p_ref[t * 4 + u // 2, 0:256, (u % 2) * HD:(u % 2 + 1) * HD] = dq.astype(BF).T

    for c in spread(0):
        c.wait_recv()
    for c in (to_x, to_p, to_m):
        c(0).start()
    row_at = lax.broadcasted_iota(jnp.int32, (SET, SLOTS), 0)
    slot_at = lax.broadcasted_iota(jnp.int32, (SET, SLOTS), 1)
    causal = (row_at <= slot_at) & (row_at < rl_ref[0, 0])

    for t in range(2):
        head = slice(t * HD, (t + 1) * HD)
        forward(t, 0, SET, RESP_AT, lambda r: r_kv[0, :, head], causal)
    w_x.wait_recv()
    w_own[1] = w_own[0] + w_in[0]
    for c in w_z:
        c.start()

    def owner_sum(t):
        z_p(t).wait_recv()
        z_m(t).wait_recv()
        x_sum(t).wait_recv()
        for i in range(2):
            total = out_buf[t, 0, i].astype(F32) + z_in[t, 0, i].astype(F32)
            total = total + (z_in[t, 1, i].astype(F32) + x_in[t, i].astype(F32))
            own[t, i] = total.astype(BF).T
        for d in (1, 2, 3):
            to_owner(t, d).start()

    def fwd_chunk(t, c):
        first = t == 0

        @pl.when(c == 0)
        def _():
            @pl.when(first)
            def _():
                to_p(0).wait_recv()
                on_p(0).start()
                to_m(0).wait_recv()
                on_m(0).start()
                to_x(0).wait_recv()
                xto_p(0).start()
                xto_m(0).start()

            put_set(t, 0)
            put_set(t, 1)

        @pl.when(c == 1)
        def _():
            @pl.when(first)
            def _():
                for w in w_z:
                    w.wait_recv()
                w_own[2] = w_own[1] + (w_in[1] + w_in[2] + w_in[3])
                for w in w_y:
                    w.start()

            @pl.when(jnp.logical_not(first))
            def _():
                owner_sum(0)

            put_set(t, 2)
            put_set(t, 3)

        @pl.when(c == 2)
        def _():
            @pl.when(first)
            def _():
                on_p(0).wait_recv()
                on_m(0).wait_recv()
                far(0).start()
                for o in spread(1):
                    o.wait_recv()
                for o in (to_x, to_p, to_m):
                    o(1).start()

            xto_p(t).wait_recv()
            xto_m(t).wait_recv()
            put_set(t, 4)
            put_set(t, 5)

        @pl.when(c == 3)
        def _():
            far(t).wait_recv()
            put_set(t, 6)
            put_set(t, 7)

        at = pl.multiple_of(c * PC, PC)
        forward(t, c + 1, PC, at, lambda r: k_n[t, pl.ds(at + r, 256), :], None)

    def finish_fwd(t):
        for u in range(QPG):
            h = t * QPG + u
            o = o_acc[h]
            total = o[HD:HD + 1, :]
            out = (o[0:HD, :] * (1.0 / total)).astype(BF)
            o_out[t * 4 + u // 2, :, (u % 2) * HD:(u % 2 + 1) * HD] = out.T
            delta[h] = jnp.sum(out.astype(F32) * d_t[h].astype(F32), 0, keepdims=True)
            lse[h] = mc[4, h] + jnp.log2(total)

    def bwd_chunk(t, c):
        first = t == 0

        @pl.when((c == 3) & first)
        def _():
            to_p(1).wait_recv()
            on_p(1).start()
            to_m(1).wait_recv()
            on_m(1).start()
            to_x(1).wait_recv()
            xto_p(1).start()
            xto_m(1).start()

        @pl.when((c == 1) & first)
        def _():
            on_p(1).wait_recv()
            on_m(1).wait_recv()
            far(1).start()

        at = pl.multiple_of(c * PC, PC)
        backward(t, c + 1, PC, at, lambda r: sets[t, 2 * c + r // SET, 1])
        for i in range(2):
            out_buf[t, 2 * c + i, 0] = dk_acc[:, i * SET:(i + 1) * SET].astype(BF)
            out_buf[t, 2 * c + i, 1] = dv_acc[:, i * SET:(i + 1) * SET].astype(BF)

        @pl.when(c == 3)
        def _():
            far_sum(t).start()

        @pl.when(c == 2)
        def _():
            plane_p(t).start()
            plane_m(t).start()
            far_sum(t).wait_recv()
            out_buf[t, 6] = (out_buf[t, 6].astype(F32) + far_in[t].astype(F32)).astype(BF)
            half_p(t).start()
            half_m(t).start()

        @pl.when(c == 0)
        def _():
            plane_p(t).wait_recv()
            plane_m(t).wait_recv()
            total = plane_in[t, 0].astype(F32) + plane_in[t, 1].astype(F32)
            out_buf[t, 3] = (out_buf[t, 3].astype(F32) + total).astype(BF)
            x_sum(t).start()
            half_p(t).wait_recv()
            out_buf[t, 2, :, :, 0:128] = (
                out_buf[t, 2, :, :, 0:128].astype(F32) + half_in[t, 0].astype(F32)
            ).astype(BF)
            z_p(t).start()
            half_m(t).wait_recv()
            out_buf[t, 1, :, :, 128:256] = (
                out_buf[t, 1, :, :, 128:256].astype(F32) + half_in[t, 1].astype(F32)
            ).astype(BF)
            z_m(t).start()

    def o_copy(i):
        return pltpu.make_async_copy(o_out.at[i], o_hbm.at[:, pair(i)], ls.at[i])

    def both(t, _):
        lax.fori_loop(0, 4, lambda c, _: (fwd_chunk(t, c), 0)[1], 0)
        finish_fwd(t)
        lax.fori_loop(0, 4, lambda i, _: (bwd_chunk(t, 3 - i), 0)[1], 0)
        return 0

    lax.fori_loop(0, 2, both, 0)
    for i in range(8):
        o_copy(i).start()
    for w in w_y:
        w.wait_recv()
    count = w_own[2] + (w_in[4] + w_in[5] + w_in[6])
    weight = (8192.0 / count)[0:1, :]
    w2 = cat([weight, weight], 1)

    for t in range(2):
        head = slice(t * HD, (t + 1) * HD)
        backward(t, 0, SET, RESP_AT, lambda r: r_kv[1, :, head])
        drk_ref[:, head] = (dk_acc[:, 0:SET] * (w2 * SCALE)).T.astype(BF)
        drv_ref[:, head] = (dv_acc[:, 0:SET] * w2).T.astype(BF)

    def dq_copy(i):
        return pltpu.make_async_copy(p_ref.at[i, 0:256, :], dq_hbm.at[:, pair(i)], ls.at[8 + i])

    query_sums(0)
    for i in range(4):
        dq_copy(i).start()
    owner_sum(1)
    query_sums(1)
    for i in range(4, 8):
        dq_copy(i).start()

    mine = lax.broadcasted_iota(jnp.int32, (64, HD), 0) + (kv * 8 + grp) * 64 < plen
    for t in range(2):
        for d in range(4):
            cols = head_cols(kvat(4 - d), t)
            if d == 0:
                got_k, got_v = own[t, 0, my_rows, :], own[t, 1, my_rows, :]
            else:
                to_owner(t, d).wait_recv()
                got_k, got_v = fin[t, d, 0], fin[t, d, 1]
            dpk_ref[:, cols] = jnp.where(mine, got_k.astype(F32) * (weight * SCALE), 0.0)
            dpv_ref[:, cols] = jnp.where(mine, got_v.astype(F32) * weight, 0.0)

    for t in range(2):
        for c in spread(t) + [g(t) for g in gather] + [s(t) for s in sums] + [to_owner(t, d) for d in (1, 2, 3)]:
            c.wait_send()
    for c in [w_x] + w_z + w_y:
        c.wait_send()
    for i in range(8):
        o_copy(i).wait()
        dq_copy(i).wait()


def hand_over(*refs):
    n = len(refs) // 2
    sems = refs[-1]
    copies = [pltpu.make_async_copy(refs[i], refs[n + i], sems.at[i]) for i in range(n)]
    for c in copies:
        c.start()
    for c in copies:
        c.wait()


def on_device(
    queries, resp_keys, resp_values, prompt_keys, prompt_values, grad_out, resp_len, prompt_len
):
    vm = pl.BlockSpec(memory_space=pltpu.VMEM)
    sm = pl.BlockSpec(memory_space=pltpu.SMEM)
    hbm = pl.BlockSpec(memory_space=pl.ANY)
    shape = jax.ShapeDtypeStruct
    dma = pltpu.SemaphoreType.DMA
    shapes = [
        shape((256, 2048), BF), shape((256, 2048), BF), shape((256, 256), BF), shape((256, 256), BF),
        shape((64, 1024), F32), shape((64, 1024), F32),
    ]
    outs = pl.pallas_call(
        kernel,
        out_shape=shapes,
        in_specs=[sm, sm] + [hbm] * 6,
        out_specs=[hbm, hbm] + [vm] * 4,
        scratch_shapes=[
            pltpu.VMEM((2, 8, 2, SET, HD), BF),
            pltpu.VMEM((HEADS, KEYS, SLOTS), BF),
            pltpu.VMEM((HEADS, KEYS, SLOTS), BF),
            pltpu.VMEM((HEADS, HD + 16, SLOTS), F32),
            pltpu.VMEM((8, SLOTS, 256), BF),
            pltpu.VMEM((5, HEADS, 1, SLOTS), F32),
            pltpu.VMEM((HEADS, 1, SLOTS), F32),
            pltpu.VMEM((HEADS, 1, SLOTS), F32),
            pltpu.VMEM((2, RESP_AT, HD), BF),
            pltpu.VMEM((2, HD, KEYS), BF),
            pltpu.VMEM((2, HD + 16, KEYS), BF),
            pltpu.VMEM((2, SET, 256), BF),
            pltpu.VMEM((HEADS, HD, SLOTS), BF),
            pltpu.VMEM((HEADS, HD, SLOTS), BF),
            pltpu.VMEM((PC, SLOTS), F32),
            pltpu.VMEM((PC, SLOTS), F32),
            pltpu.VMEM((PC, SLOTS), BF),
            pltpu.VMEM((PC, SLOTS), BF),
            pltpu.VMEM((HD, SLOTS), BF),
            pltpu.VMEM((HD, SLOTS), BF),
            pltpu.VMEM((HD, PC), F32),
            pltpu.VMEM((HD, PC), F32),
            pltpu.VMEM((2, 8, 2, HD, SET), BF),
            pltpu.VMEM((2, 2, SET, HD), BF),
            pltpu.VMEM((2, 2, 2, HD, 128), BF),
            pltpu.VMEM((2, 2, 2, HD, SET), BF),
            pltpu.VMEM((2, 2, 2, HD, SET), BF),
            pltpu.VMEM((2, 2, HD, SET), BF),
            pltpu.VMEM((2, 2, HD, SET), BF),
            pltpu.VMEM((2, 4, 2, 64, HD), BF),
            pltpu.VMEM((3, 8, 128), F32),
            pltpu.VMEM((7, 8, 128), F32),
            dma((22,)), dma((2, 6)), dma((2, 6)), dma((2, 8)), dma((2, 8)), dma((2, 8)), dma((2, 8)),
            dma((2, 4)), dma((2, 4)), dma((7,)), dma((7,)),
        ],
        compiler_params=pltpu.CompilerParams(
            collective_id=0, has_side_effects=True, vmem_limit_bytes=62 * 2**20
        ),
        name="attention",
    )(
        resp_len, prompt_len, queries.reshape(256, 2048), grad_out.reshape(256, 2048),
        resp_keys.reshape(256, 256), resp_values.reshape(256, 256),
        prompt_keys.reshape(64, 1024), prompt_values.reshape(64, 1024),
    )
    attended, grad_q, grad_rk, grad_rv, grad_pk, grad_pv = pl.pallas_call(
        hand_over,
        out_shape=shapes,
        in_specs=[hbm] * 6,
        out_specs=[hbm] * 6,
        scratch_shapes=[dma((6,))],
        name="hand_over",
    )(*outs)
    return (
        attended.reshape(queries.shape),
        grad_q.reshape(queries.shape),
        grad_rk.reshape(resp_keys.shape),
        grad_rv.reshape(resp_values.shape),
        grad_pk.reshape(1, 64, 1024),
        grad_pv.reshape(1, 64, 1024),
    )


def solution(mesh):
    wide = P("prompt", "grp", None, "kv")
    rows = P("prompt", ("kv", "grp"), None)
    return jax.shard_map(
        on_device,
        mesh=mesh,
        in_specs=(wide, wide, wide, rows, rows, wide, P("prompt", "grp"), P("prompt")),
        out_specs=(wide, wide, wide, wide, rows, rows),
        check_vma=False,
    )
```

time: 81.8 us -> 162 us (1.98)
  Pallas kernels: 73.1 us -> 160 us
  local copies, waits for them, and re-layouts: 6.46 us -> 0 us
    pallas_call x1 -> x2, Pallas kernels: 73.1 us -> 160 us  [the longest x1 88.5 us: on_device(): pl.pallas_call(hand_over, out_shape=shapes, in_specs=[hbm] * 6, out_specs...]
    unnamed x16 -> x0, local copies, waits for them, and re-layouts: 6.46 us -> none
where the time goes in v3:
time: 162 us; the launch traced here: 161 us
  Pallas kernels  160 us (99%)
  between operations  1.93 us (1%)
    pallas_call x1, Pallas kernels, on_device(): pl.pallas_call(hand_over, out_shape=shapes, in_specs=[hbm] * 6, out_specs...  88.5 us
    pallas_call x1, Pallas kernels, on_device(): pl.pallas_call(kernel, out_shape=shapes, in_specs=[sm, sm] + [hbm] * 6, o...  71 us

profile of v3, /device:TPU:1, one launch (start us, length us, event | category | flops | bytes accessed | tf_op | source)
XLA Modules:
  0.0 161.4 jit_solution(13977370557393670668)
XLA Ops:
  1.9 71.0 %attention.1 = (bf16[256,2048]{1,0:T(8,128)(2,1)}, bf16[256,2048]{1,0:T(8,128)(2,1)}, bf16[256,256]{1,0:T(8,128)(2,1)}, bf16[256,256]{1,0:T(8,128)(2,1)}, f32[64,1024]{1,0:T(8,128)}, /*index=5*/f32[64,1024]{1,0:T(8,128)}) custom-call(s32[1,1]{1,0:T(1,128)S(6)} %copy.14.rl_ref, s32[1]{0:T(128)S(6)} %copy.15.pl_ref, bf16[256,2048]{1,0:T(8,128)(2,1)} %bitcast.12, ...), custom_call_target="tpu_custom_call" | custom-call | tf_op jit(solution)/shard_map/attention/pallas_call | solution.py:480
  72.9 88.5 %hand_over.1 = (bf16[256,2048]{1,0:T(8,128)(2,1)}, bf16[256,2048]{1,0:T(8,128)(2,1)}, bf16[256,256]{1,0:T(8,128)(2,1)}, bf16[256,256]{1,0:T(8,128)(2,1)}, f32[64,1024]{1,0:T(8,128)}, /*index=5*/f32[64,1024]{1,0:T(8,128)}) custom-call(bf16[256,2048]{1,0:T(8,128)(2,1)} %get-tuple-element.18.refs_0_, bf16[256,2048]{1,0:T(8,128)(2,1)} %get-tuple-element.19.refs_1_, ...), custom_call_target="tpu_custom_call" | custom-call | tf_op jit(solution)/shard_map/hand_over/pallas_call | solution.py:530

commit v4 on v3

--- a/solution.py
+++ b/solution.py
@@ -20,7 +20,9 @@
 SLOTS = 256
 RESP_AT = 2048
 KEYS = 2304
-SETS = ((0, 0), (0, 3), (0, 1), (1, 0), (1, 1), (1, 3), (0, 2), (1, 2))
+OWN_AT = 1792
+LAST_AT = 1536
+SETS = ((0, 0), (0, 3), (0, 1), (1, 0), (0, 2), (1, 1), (1, 3), (1, 2))
 
 
 def dot(a, b, dims):
@@ -56,15 +58,13 @@
     for i in range(8):
         local.append(pltpu.make_async_copy(q_hbm.at[:, pair(i)], ds_ref.at[i, 0:256, :], ls.at[i]))
         local.append(pltpu.make_async_copy(do_hbm.at[:, pair(i)], ds_ref.at[i, 256:512, :], ls.at[8 + i]))
-    local.append(pltpu.make_async_copy(rk_hbm, r_kv.at[0], ls.at[16]))
-    local.append(pltpu.make_async_copy(rv_hbm, r_kv.at[1], ls.at[17]))
     for t in range(2):
         for i, ref in ((0, pk_hbm), (1, pv_hbm)):
-            local.append(
-                pltpu.make_async_copy(
-                    ref.at[:, head_cols(kv, t)], sets.at[t, 0, i, my_rows, :], ls.at[18 + t * 2 + i]
-                )
-            )
+            n = 16 + t * 2 + i
+            local.append(pltpu.make_async_copy(ref.at[:, head_cols(kv, t)], sets.at[t, 0, i, my_rows, :], ls.at[n]))
+        for i, ref in ((0, rk_hbm), (1, rv_hbm)):
+            n = 20 + t * 2 + i
+            local.append(pltpu.make_async_copy(ref.at[:, t * HD:(t + 1) * HD], r_kv.at[i, t], ls.at[n]))
     for c in local:
         c.start()
 
@@ -102,11 +102,11 @@
     to_x = lambda t: moved(t, 0, 0, 3, xp)
     to_p = lambda t: moved(t, 1, 0, 1, zp)
     to_m = lambda t: moved(t, 2, 0, 2, zm)
-    on_p = lambda t: moved(t, 3, 1, 6, zp, lo)
-    on_m = lambda t: moved(t, 4, 2, 6, zm, hi)
-    xto_p = lambda t: moved(t, 5, 3, 5, zp)
-    xto_m = lambda t: moved(t, 6, 3, 4, zm)
-    far = lambda t: moved(t, 7, 6, 7, xp)
+    on_p = lambda t: moved(t, 3, 1, 4, zp, lo)
+    on_m = lambda t: moved(t, 4, 2, 4, zm, hi)
+    xto_p = lambda t: moved(t, 5, 3, 6, zp)
+    xto_m = lambda t: moved(t, 6, 3, 5, zm)
+    far = lambda t: moved(t, 7, 4, 7, xp)
     gather = [to_x, to_p, to_m, on_p, on_m, xto_p, xto_m, far]
     w_x = cp(w_own.at[0], w_in.at[0], ws.at[0], wr.at[0], xp)
     w_z = [cp(w_own.at[1], w_in.at[d], ws.at[d], wr.at[d], zat(d)) for d in (1, 2, 3)]
@@ -115,10 +115,10 @@
         return cp(src, dst, hs.at[t, n], hr.at[t, n], dev)
 
     far_sum = lambda t: summed(t, 0, out_buf.at[t, 7], far_in.at[t], xp)
-    half_p = lambda t: summed(t, 1, out_buf.at[t, 6, :, :, lo], half_in.at[t, 0], zp)
-    half_m = lambda t: summed(t, 2, out_buf.at[t, 6, :, :, hi], half_in.at[t, 1], zm)
-    plane_p = lambda t: summed(t, 3, out_buf.at[t, 4], plane_in.at[t, 0], zp)
-    plane_m = lambda t: summed(t, 4, out_buf.at[t, 5], plane_in.at[t, 1], zm)
+    half_p = lambda t: summed(t, 1, out_buf.at[t, 4, :, :, lo], half_in.at[t, 0], zp)
+    half_m = lambda t: summed(t, 2, out_buf.at[t, 4, :, :, hi], half_in.at[t, 1], zm)
+    plane_p = lambda t: summed(t, 3, out_buf.at[t, 5], plane_in.at[t, 0], zp)
+    plane_m = lambda t: summed(t, 4, out_buf.at[t, 6], plane_in.at[t, 1], zm)
     z_p = lambda t: summed(t, 5, out_buf.at[t, 2], z_in.at[t, 0], zp)
     z_m = lambda t: summed(t, 6, out_buf.at[t, 1], z_in.at[t, 1], zm)
     x_sum = lambda t: summed(t, 7, out_buf.at[t, 3], x_in.at[t], xp)
@@ -128,9 +128,8 @@
         rows = pl.ds(pl.multiple_of(kvat(d) * 64, 64), 64)
         return cp(own.at[t, :, rows, :], fin.at[t, d], ks.at[t, d], kr.at[t, d], {"kv": kvat(d)})
 
-    for t in range(2):
-        for c in spread(t):
-            c.start()
+    for c in spread(0):
+        c.start()
     w_own[0] = jnp.full((8, 128), rl_ref[0, 0].astype(F32))
     w_x.start()
     for c in local:
@@ -149,9 +148,9 @@
 
     lax.fori_loop(0, HEADS // 4, stage_queries, 0)
     for t in range(2):
-        head = slice(t * HD, (t + 1) * HD)
-        k_t[t, :, RESP_AT:] = r_kv[0, :, head].T
-        v_t[t, 0:HD, RESP_AT:] = r_kv[1, :, head].T
+        k_n[t, RESP_AT:, :] = r_kv[0, t]
+        k_t[t, :, RESP_AT:] = r_kv[0, t].T
+        v_t[t, 0:HD, RESP_AT:] = r_kv[1, t].T
         v_t[t, HD:, RESP_AT:] = jnp.ones((16, SET), BF)
 
     plen = pl_ref[0]
@@ -165,7 +164,8 @@
     def put_set(t, s):
         by_row = valid_keys(s, (SET, HD), 0)
         by_col = valid_keys(s, (16, SET), 1)
-        at = slice(s * SET, (s + 1) * SET)
+        start = (s - 1) * SET if s else OWN_AT
+        at = slice(start, start + SET)
         k = sets[t, s, 0]
         k_n[t, at, :] = k * by_row + k[0:1, :] * (1 - by_row)
         k_t[t, :, at] = k.T * by_col[0:1, :]
@@ -174,13 +174,13 @@
 
     s_bufs, ds_bufs, dc_bufs = (s_a, s_b), (ds_a, ds_b), (dc_a, dc_b)
 
-    def scores(t, j, u, rows, keys, mask):
+    def scores(t, j, u, rows, at, mask):
         h = t * QPG + u
         s_ref = s_bufs[u % 2]
         top = None
         for r in range(0, rows, 256):
-            s = dot(keys(r), q_t[h], NN) * (SCALE * LOG2E)
-            if mask is not None:
+            s = dot(k_n[t, pl.ds(at + r, 256), :], q_t[h], NN) * (SCALE * LOG2E)
+            if mask is not None and r:
                 s = jnp.where(mask, s, -1e30)
             s_ref[r:r + 256, :] = s
             b = jnp.max(s.reshape(32, 8, SLOTS), 0)
@@ -200,10 +200,10 @@
         new = dot(v_t[t, :, pl.ds(at, rows)], cat(parts, 0), NN)
         o_acc[h] = new if first else o_acc[h] * jnp.exp2(mc[j - 1, h] - m) + new
 
-    def forward(t, j, rows, at, keys, mask):
+    def forward(t, j, rows, at, mask):
         for u in range(QPG + 1):
             if u < QPG:
-                scores(t, j, u, rows, keys, mask)
+                scores(t, j, u, rows, at, mask)
             if u > 0:
                 attend(t, j, u - 1, rows, at, mask is not None)
 
@@ -248,13 +248,23 @@
         c.wait_recv()
     for c in (to_x, to_p, to_m):
         c(0).start()
+    for c in spread(1):
+        c.start()
     row_at = lax.broadcasted_iota(jnp.int32, (SET, SLOTS), 0)
     slot_at = lax.broadcasted_iota(jnp.int32, (SET, SLOTS), 1)
     causal = (row_at <= slot_at) & (row_at < rl_ref[0, 0])
 
-    for t in range(2):
-        head = slice(t * HD, (t + 1) * HD)
-        forward(t, 0, SET, RESP_AT, lambda r: r_kv[0, :, head], causal)
+    def first_chunk(t, _):
+        @pl.when(t == 1)
+        def _():
+            for c in spread(1):
+                c.wait_recv()
+
+        put_set(t, 0)
+        forward(t, 0, PC, OWN_AT, causal)
+        return 0
+
+    lax.fori_loop(0, 2, first_chunk, 0)
     w_x.wait_recv()
     w_own[1] = w_own[0] + w_in[0]
     for c in w_z:
@@ -271,10 +281,35 @@
         for d in (1, 2, 3):
             to_owner(t, d).start()
 
+    def plane_sums(t):
+        plane_p(t).wait_recv()
+        plane_m(t).wait_recv()
+        total = plane_in[t, 0].astype(F32) + plane_in[t, 1].astype(F32)
+        out_buf[t, 3] = (out_buf[t, 3].astype(F32) + total).astype(BF)
+        x_sum(t).start()
+
+    def half_sums(t):
+        half_p(t).wait_recv()
+        out_buf[t, 2, :, :, 0:128] = (
+            out_buf[t, 2, :, :, 0:128].astype(F32) + half_in[t, 0].astype(F32)
+        ).astype(BF)
+        z_p(t).start()
+        half_m(t).wait_recv()
+        out_buf[t, 1, :, :, 128:256] = (
+            out_buf[t, 1, :, :, 128:256].astype(F32) + half_in[t, 1].astype(F32)
+        ).astype(BF)
+        z_m(t).start()
+
+    def far_sums(t):
+        far_sum(t).wait_recv()
+        out_buf[t, 4] = (out_buf[t, 4].astype(F32) + far_in[t].astype(F32)).astype(BF)
+        half_p(t).start()
+        half_m(t).start()
+
     def fwd_chunk(t, c):
         first = t == 0
 
-        @pl.when(c == 0)
+        @pl.when(c == 1)
         def _():
             @pl.when(first)
             def _():
@@ -286,13 +321,16 @@
                 xto_p(0).start()
                 xto_m(0).start()
 
-            put_set(t, 0)
             put_set(t, 1)
-
-        @pl.when(c == 1)
+            put_set(t, 2)
+
+        @pl.when(c == 2)
         def _():
             @pl.when(first)
             def _():
+                on_p(0).wait_recv()
+                on_m(0).wait_recv()
+                far(0).start()
                 for w in w_z:
                     w.wait_recv()
                 w_own[2] = w_own[1] + (w_in[1] + w_in[2] + w_in[3])
@@ -301,36 +339,29 @@
 
             @pl.when(jnp.logical_not(first))
             def _():
-                owner_sum(0)
-
-            put_set(t, 2)
+                plane_sums(0)
+
             put_set(t, 3)
-
-        @pl.when(c == 2)
-        def _():
+            put_set(t, 4)
+
+        @pl.when(c == 3)
+        def _():
+            xto_p(t).wait_recv()
+            xto_m(t).wait_recv()
+
             @pl.when(first)
             def _():
-                on_p(0).wait_recv()
-                on_m(0).wait_recv()
-                far(0).start()
-                for o in spread(1):
-                    o.wait_recv()
                 for o in (to_x, to_p, to_m):
                     o(1).start()
 
-            xto_p(t).wait_recv()
-            xto_m(t).wait_recv()
-            put_set(t, 4)
+            @pl.when(jnp.logical_not(first))
+            def _():
+                half_sums(0)
+
             put_set(t, 5)
-
-        @pl.when(c == 3)
-        def _():
-            far(t).wait_recv()
             put_set(t, 6)
-            put_set(t, 7)
-
-        at = pl.multiple_of(c * PC, PC)
-        forward(t, c + 1, PC, at, lambda r: k_n[t, pl.ds(at + r, 256), :], None)
+
+        forward(t, c, PC, pl.multiple_of((c - 1) * PC, PC), None)
 
     def finish_fwd(t):
         for u in range(QPG):
@@ -342,6 +373,11 @@
             delta[h] = jnp.sum(out.astype(F32) * d_t[h].astype(F32), 0, keepdims=True)
             lse[h] = mc[4, h] + jnp.log2(total)
 
+    def put_out(t, s, i):
+        cols = slice(i * SET, (i + 1) * SET)
+        out_buf[t, s, 0] = dk_acc[:, cols].astype(BF)
+        out_buf[t, s, 1] = dv_acc[:, cols].astype(BF)
+
     def bwd_chunk(t, c):
         first = t == 0
 
@@ -361,50 +397,39 @@
             on_m(1).wait_recv()
             far(1).start()
 
-        at = pl.multiple_of(c * PC, PC)
-        backward(t, c + 1, PC, at, lambda r: sets[t, 2 * c + r // SET, 1])
-        for i in range(2):
-            out_buf[t, 2 * c + i, 0] = dk_acc[:, i * SET:(i + 1) * SET].astype(BF)
-            out_buf[t, 2 * c + i, 1] = dv_acc[:, i * SET:(i + 1) * SET].astype(BF)
+        backward(t, c, PC, pl.multiple_of((c - 1) * PC, PC), lambda r: sets[t, 2 * c - 1 + r // SET, 1])
+        put_out(t, 2 * c - 1, 0)
+        put_out(t, 2 * c, 1)
 
         @pl.when(c == 3)
-        def _():
-            far_sum(t).start()
-
-        @pl.when(c == 2)
         def _():
             plane_p(t).start()
             plane_m(t).start()
-            far_sum(t).wait_recv()
-            out_buf[t, 6] = (out_buf[t, 6].astype(F32) + far_in[t].astype(F32)).astype(BF)
-            half_p(t).start()
-            half_m(t).start()
-
-        @pl.when(c == 0)
-        def _():
-            plane_p(t).wait_recv()
-            plane_m(t).wait_recv()
-            total = plane_in[t, 0].astype(F32) + plane_in[t, 1].astype(F32)
-            out_buf[t, 3] = (out_buf[t, 3].astype(F32) + total).astype(BF)
-            x_sum(t).start()
-            half_p(t).wait_recv()
-            out_buf[t, 2, :, :, 0:128] = (
-                out_buf[t, 2, :, :, 0:128].astype(F32) + half_in[t, 0].astype(F32)
-            ).astype(BF)
-            z_p(t).start()
-            half_m(t).wait_recv()
-            out_buf[t, 1, :, :, 128:256] = (
-                out_buf[t, 1, :, :, 128:256].astype(F32) + half_in[t, 1].astype(F32)
-            ).astype(BF)
-            z_m(t).start()
+
+        @pl.when(c == 1)
+        def _():
+            far_sums(t)
+
+    def own_chunk(t):
+        backward(t, 0, PC, OWN_AT, lambda r: sets[t, 0, 1] if r == 0 else r_kv[1, t])
+        put_out(t, 0, 0)
+        head = slice(t * HD, (t + 1) * HD)
+        drk_ref[:, head] = (dk_acc[:, SET:] * (w2 * SCALE)).T.astype(BF)
+        drv_ref[:, head] = (dv_acc[:, SET:] * w2).T.astype(BF)
 
     def o_copy(i):
         return pltpu.make_async_copy(o_out.at[i], o_hbm.at[:, pair(i)], ls.at[i])
 
     def both(t, _):
-        lax.fori_loop(0, 4, lambda c, _: (fwd_chunk(t, c), 0)[1], 0)
+        lax.fori_loop(1, 4, lambda c, _: (fwd_chunk(t, c), 0)[1], 0)
+        far(t).wait_recv()
+        put_set(t, 7)
+        forward(t, 4, SET, LAST_AT, None)
         finish_fwd(t)
-        lax.fori_loop(0, 4, lambda i, _: (bwd_chunk(t, 3 - i), 0)[1], 0)
+        backward(t, 4, SET, LAST_AT, lambda r: sets[t, 7, 1])
+        put_out(t, 7, 0)
+        far_sum(t).start()
+        lax.fori_loop(0, 3, lambda i, _: (bwd_chunk(t, 3 - i), 0)[1], 0)
         return 0
 
     lax.fori_loop(0, 2, both, 0)
@@ -416,22 +441,20 @@
     weight = (8192.0 / count)[0:1, :]
     w2 = cat([weight, weight], 1)
 
-    for t in range(2):
-        head = slice(t * HD, (t + 1) * HD)
-        backward(t, 0, SET, RESP_AT, lambda r: r_kv[1, :, head])
-        drk_ref[:, head] = (dk_acc[:, 0:SET] * (w2 * SCALE)).T.astype(BF)
-        drv_ref[:, head] = (dv_acc[:, 0:SET] * w2).T.astype(BF)
+    own_chunk(1)
+    plane_sums(1)
+    half_sums(1)
+    own_chunk(0)
+    owner_sum(0)
 
     def dq_copy(i):
         return pltpu.make_async_copy(p_ref.at[i, 0:256, :], dq_hbm.at[:, pair(i)], ls.at[8 + i])
 
-    query_sums(0)
-    for i in range(4):
-        dq_copy(i).start()
+    for t in range(2):
+        query_sums(t)
+        for i in range(t * 4, t * 4 + 4):
+            dq_copy(i).start()
     owner_sum(1)
-    query_sums(1)
-    for i in range(4, 8):
-        dq_copy(i).start()
 
     mine = lax.broadcasted_iota(jnp.int32, (64, HD), 0) + (kv * 8 + grp) * 64 < plen
     for t in range(2):
@@ -491,10 +514,10 @@
             pltpu.VMEM((5, HEADS, 1, SLOTS), F32),
             pltpu.VMEM((HEADS, 1, SLOTS), F32),
             pltpu.VMEM((HEADS, 1, SLOTS), F32),
-            pltpu.VMEM((2, RESP_AT, HD), BF),
+            pltpu.VMEM((2, KEYS, HD), BF),
             pltpu.VMEM((2, HD, KEYS), BF),
             pltpu.VMEM((2, HD + 16, KEYS), BF),
-            pltpu.VMEM((2, SET, 256), BF),
+            pltpu.VMEM((2, 2, SET, HD), BF),
             pltpu.VMEM((HEADS, HD, SLOTS), BF),
             pltpu.VMEM((HEADS, HD, SLOTS), BF),
             pltpu.VMEM((PC, SLOTS), F32),
@@ -515,7 +538,7 @@
             pltpu.VMEM((2, 4, 2, 64, HD), BF),
             pltpu.VMEM((3, 8, 128), F32),
             pltpu.VMEM((7, 8, 128), F32),
-            dma((22,)), dma((2, 6)), dma((2, 6)), dma((2, 8)), dma((2, 8)), dma((2, 8)), dma((2, 8)),
+            dma((24,)), dma((2, 6)), dma((2, 6)), dma((2, 8)), dma((2, 8)), dma((2, 8)), dma((2, 8)),
             dma((2, 4)), dma((2, 4)), dma((7,)), dma((7,)),
         ],
         compiler_params=pltpu.CompilerParams(
@@ -530,7 +553,7 @@
     attended, grad_q, grad_rk, grad_rv, grad_pk, grad_pv = pl.pallas_call(
         hand_over,
         out_shape=shapes,
-        in_specs=[hbm] * 6,
+        in_specs=[vm] * 6,
         out_specs=[hbm] * 6,
         scratch_shapes=[dma((6,))],
         name="hand_over",

time: 162 us -> 70.1 us (0.43)
  Pallas kernels: 160 us -> 67.8 us
    pallas_call x1, Pallas kernels: 88.5 us -> 3.36 us  [on_device(): pl.pallas_call(hand_over, out_shape=shapes, in_specs=[vm] * 6, out_specs=...]
    pallas_call x1, Pallas kernels: 71 us -> 64.5 us  [on_device(): pl.pallas_call(kernel, out_shape=shapes, in_specs=[sm, sm] + [hbm] * 6, o...]
where the time goes in v4:
time: 70.1 us; the launch traced here: 69.9 us
  Pallas kernels  67.8 us (97%)
  between operations  2.09 us (3%)
    pallas_call x1, Pallas kernels, on_device(): pl.pallas_call(kernel, out_shape=shapes, in_specs=[sm, sm] + [hbm] * 6, o...  64.5 us
    pallas_call x1, Pallas kernels, on_device(): pl.pallas_call(hand_over, out_shape=shapes, in_specs=[vm] * 6, out_specs=...  3.36 us

profile of v4, /device:TPU:1, one launch (start us, length us, event | category | flops | bytes accessed | tf_op | source)
XLA Modules:
  0.0 69.9 jit_solution(9261290226860274360)
XLA Ops:
  1.9 64.5 %attention.1 = (bf16[256,2048]{1,0:T(8,128)(2,1)}, bf16[256,2048]{1,0:T(8,128)(2,1)}, bf16[256,256]{1,0:T(8,128)(2,1)}, bf16[256,256]{1,0:T(8,128)(2,1)}, f32[64,1024]{1,0:T(8,128)}, /*index=5*/f32[64,1024]{1,0:T(8,128)}) custom-call(s32[1,1]{1,0:T(1,128)S(6)} %copy.14.rl_ref, s32[1]{0:T(128)S(6)} %copy.15.pl_ref, bf16[256,2048]{1,0:T(8,128)(2,1)} %bitcast.12, ...), custom_call_target="tpu_custom_call" | custom-call | tf_op jit(solution)/shard_map/attention/pallas_call | solution.py:503
  66.4 3.4 %hand_over.1 = (bf16[256,2048]{1,0:T(8,128)(2,1)}, bf16[256,2048]{1,0:T(8,128)(2,1)}, bf16[256,256]{1,0:T(8,128)(2,1)}, bf16[256,256]{1,0:T(8,128)(2,1)}, f32[64,1024]{1,0:T(8,128)}, /*index=5*/f32[64,1024]{1,0:T(8,128)}) custom-call(bf16[256,2048]{1,0:T(8,128)(2,1)} %get-tuple-element.18.refs_0_, bf16[256,2048]{1,0:T(8,128)(2,1)} %get-tuple-element.19.refs_1_, ...), custom_call_target="tpu_custom_call" | custom-call | tf_op jit(solution)/shard_map/hand_over/pallas_call | solution.py:553

commit v5 on v4

--- a/solution.py
+++ b/solution.py
@@ -80,56 +80,54 @@
             src_ref=src, dst_ref=dst, send_sem=ssem, recv_sem=rsem, device_id=dev, device_id_type=MESH
         )
 
-    def spread(t):
-        made = []
-        for d in (1, 2, 3):
-            for i, ref in ((0, pk_hbm), (1, pv_hbm)):
-                n = (d - 1) * 2 + i
-                made.append(
-                    cp(ref.at[:, head_cols(kvat(d), t)], sets.at[t, 0, i, my_rows, :],
-                       a2a_s.at[t, n], a2a_r.at[t, n], {"kv": kvat(d)})
-                )
-        return made
+    def spread(t, i):
+        ref = (pk_hbm, pv_hbm)[i]
+        return [
+            cp(ref.at[:, head_cols(kvat(d), t)], sets.at[t, 0, i, my_rows, :],
+               a2a_s.at[t, i, d], a2a_r.at[t, i, d], {"kv": kvat(d)})
+            for d in (1, 2, 3)
+        ]
 
     lo, hi = pl.ds(0, 128), pl.ds(128, 128)
 
-    def moved(t, n, src, dst, dev, rows=None):
-        a, b = sets.at[t, src], sets.at[t, dst]
+    def moved(t, i, n, src, dst, dev, rows=None):
+        a, b = sets.at[t, src, i], sets.at[t, dst, i]
         if rows is not None:
-            a, b = a.at[:, rows], b.at[:, rows]
-        return cp(a, b, gs.at[t, n], gr.at[t, n], dev)
-
-    to_x = lambda t: moved(t, 0, 0, 3, xp)
-    to_p = lambda t: moved(t, 1, 0, 1, zp)
-    to_m = lambda t: moved(t, 2, 0, 2, zm)
-    on_p = lambda t: moved(t, 3, 1, 4, zp, lo)
-    on_m = lambda t: moved(t, 4, 2, 4, zm, hi)
-    xto_p = lambda t: moved(t, 5, 3, 6, zp)
-    xto_m = lambda t: moved(t, 6, 3, 5, zm)
-    far = lambda t: moved(t, 7, 4, 7, xp)
+            a, b = a.at[rows], b.at[rows]
+        return cp(a, b, gs.at[t, i, n], gr.at[t, i, n], dev)
+
+    to_x = lambda t, i: moved(t, i, 0, 0, 3, xp)
+    to_p = lambda t, i: moved(t, i, 1, 0, 1, zp)
+    to_m = lambda t, i: moved(t, i, 2, 0, 2, zm)
+    on_p = lambda t, i: moved(t, i, 3, 1, 4, zp, lo)
+    on_m = lambda t, i: moved(t, i, 4, 2, 4, zm, hi)
+    xto_p = lambda t, i: moved(t, i, 5, 3, 6, zp)
+    xto_m = lambda t, i: moved(t, i, 6, 3, 5, zm)
+    far = lambda t, i: moved(t, i, 7, 4, 7, xp)
     gather = [to_x, to_p, to_m, on_p, on_m, xto_p, xto_m, far]
     w_x = cp(w_own.at[0], w_in.at[0], ws.at[0], wr.at[0], xp)
     w_z = [cp(w_own.at[1], w_in.at[d], ws.at[d], wr.at[d], zat(d)) for d in (1, 2, 3)]
     w_y = [cp(w_own.at[2], w_in.at[3 + d], ws.at[3 + d], wr.at[3 + d], yat(d)) for d in (1, 2, 3)]
-    def summed(t, n, src, dst, dev):
-        return cp(src, dst, hs.at[t, n], hr.at[t, n], dev)
-
-    far_sum = lambda t: summed(t, 0, out_buf.at[t, 7], far_in.at[t], xp)
-    half_p = lambda t: summed(t, 1, out_buf.at[t, 4, :, :, lo], half_in.at[t, 0], zp)
-    half_m = lambda t: summed(t, 2, out_buf.at[t, 4, :, :, hi], half_in.at[t, 1], zm)
-    plane_p = lambda t: summed(t, 3, out_buf.at[t, 5], plane_in.at[t, 0], zp)
-    plane_m = lambda t: summed(t, 4, out_buf.at[t, 6], plane_in.at[t, 1], zm)
-    z_p = lambda t: summed(t, 5, out_buf.at[t, 2], z_in.at[t, 0], zp)
-    z_m = lambda t: summed(t, 6, out_buf.at[t, 1], z_in.at[t, 1], zm)
-    x_sum = lambda t: summed(t, 7, out_buf.at[t, 3], x_in.at[t], xp)
+    def summed(t, i, n, src, dst, dev):
+        return cp(src, dst, hs.at[t, i, n], hr.at[t, i, n], dev)
+
+    far_sum = lambda t, i: summed(t, i, 0, out_buf.at[t, 7, i], far_in.at[t, i], xp)
+    half_p = lambda t, i: summed(t, i, 1, out_buf.at[t, 4, i, :, lo], half_in.at[t, 0, i], zp)
+    half_m = lambda t, i: summed(t, i, 2, out_buf.at[t, 4, i, :, hi], half_in.at[t, 1, i], zm)
+    plane_p = lambda t, i: summed(t, i, 3, out_buf.at[t, 5, i], plane_in.at[t, 0, i], zp)
+    plane_m = lambda t, i: summed(t, i, 4, out_buf.at[t, 6, i], plane_in.at[t, 1, i], zm)
+    z_p = lambda t, i: summed(t, i, 5, out_buf.at[t, 2, i], z_in.at[t, 0, i], zp)
+    z_m = lambda t, i: summed(t, i, 6, out_buf.at[t, 1, i], z_in.at[t, 1, i], zm)
+    x_sum = lambda t, i: summed(t, i, 7, out_buf.at[t, 3, i], x_in.at[t, i], xp)
     sums = [far_sum, half_p, half_m, plane_p, plane_m, z_p, z_m, x_sum]
 
-    def to_owner(t, d):
+    def to_owner(t, i, d):
         rows = pl.ds(pl.multiple_of(kvat(d) * 64, 64), 64)
-        return cp(own.at[t, :, rows, :], fin.at[t, d], ks.at[t, d], kr.at[t, d], {"kv": kvat(d)})
-
-    for c in spread(0):
-        c.start()
+        return cp(own.at[t, i, rows, :], fin.at[t, d, i], ks.at[t, i, d], kr.at[t, i, d], {"kv": kvat(d)})
+
+    for i in range(2):
+        for c in spread(0, i):
+            c.start()
     w_own[0] = jnp.full((8, 128), rl_ref[0, 0].astype(F32))
     w_x.start()
     for c in local:
@@ -244,82 +242,89 @@
             dq = dot(k_t[t], ds_ref[h], NN) * (w2 * SCALE)
             p_ref[t * 4 + u // 2, 0:256, (u % 2) * HD:(u % 2 + 1) * HD] = dq.astype(BF).T
 
-    for c in spread(0):
-        c.wait_recv()
-    for c in (to_x, to_p, to_m):
-        c(0).start()
-    for c in spread(1):
-        c.start()
+    for i in range(2):
+        for c in spread(0, i):
+            c.wait_recv()
+        for c in (to_x, to_p, to_m):
+            c(0, i).start()
     row_at = lax.broadcasted_iota(jnp.int32, (SET, SLOTS), 0)
     slot_at = lax.broadcasted_iota(jnp.int32, (SET, SLOTS), 1)
     causal = (row_at <= slot_at) & (row_at < rl_ref[0, 0])
 
-    def first_chunk(t, _):
-        @pl.when(t == 1)
-        def _():
-            for c in spread(1):
-                c.wait_recv()
-
+    def first_chunk(t):
         put_set(t, 0)
         forward(t, 0, PC, OWN_AT, causal)
-        return 0
-
-    lax.fori_loop(0, 2, first_chunk, 0)
+
+    first_chunk(0)
     w_x.wait_recv()
     w_own[1] = w_own[0] + w_in[0]
     for c in w_z:
         c.start()
 
+    def pass_on(t):
+        for i in range(2):
+            to_p(t, i).wait_recv()
+            on_p(t, i).start()
+            to_m(t, i).wait_recv()
+            on_m(t, i).start()
+            to_x(t, i).wait_recv()
+            xto_p(t, i).start()
+            xto_m(t, i).start()
+
+    def pass_far(t):
+        for i in range(2):
+            on_p(t, i).wait_recv()
+            on_m(t, i).wait_recv()
+            far(t, i).start()
+
     def owner_sum(t):
-        z_p(t).wait_recv()
-        z_m(t).wait_recv()
-        x_sum(t).wait_recv()
         for i in range(2):
+            z_p(t, i).wait_recv()
+            z_m(t, i).wait_recv()
+            x_sum(t, i).wait_recv()
             total = out_buf[t, 0, i].astype(F32) + z_in[t, 0, i].astype(F32)
             total = total + (z_in[t, 1, i].astype(F32) + x_in[t, i].astype(F32))
             own[t, i] = total.astype(BF).T
-        for d in (1, 2, 3):
-            to_owner(t, d).start()
-
-    def plane_sums(t):
-        plane_p(t).wait_recv()
-        plane_m(t).wait_recv()
-        total = plane_in[t, 0].astype(F32) + plane_in[t, 1].astype(F32)
-        out_buf[t, 3] = (out_buf[t, 3].astype(F32) + total).astype(BF)
-        x_sum(t).start()
-
-    def half_sums(t):
-        half_p(t).wait_recv()
-        out_buf[t, 2, :, :, 0:128] = (
-            out_buf[t, 2, :, :, 0:128].astype(F32) + half_in[t, 0].astype(F32)
+            for d in (1, 2, 3):
+                to_owner(t, i, d).start()
+
+    def plane_sums(t, i):
+        plane_p(t, i).wait_recv()
+        plane_m(t, i).wait_recv()
+        total = plane_in[t, 0, i].astype(F32) + plane_in[t, 1, i].astype(F32)
+        out_buf[t, 3, i] = (out_buf[t, 3, i].astype(F32) + total).astype(BF)
+        x_sum(t, i).start()
+
+    def half_sums(t, i):
+        half_p(t, i).wait_recv()
+        out_buf[t, 2, i, :, 0:128] = (
+            out_buf[t, 2, i, :, 0:128].astype(F32) + half_in[t, 0, i].astype(F32)
         ).astype(BF)
-        z_p(t).start()
-        half_m(t).wait_recv()
-        out_buf[t, 1, :, :, 128:256] = (
-            out_buf[t, 1, :, :, 128:256].astype(F32) + half_in[t, 1].astype(F32)
+        z_p(t, i).start()
+        half_m(t, i).wait_recv()
+        out_buf[t, 1, i, :, 128:256] = (
+            out_buf[t, 1, i, :, 128:256].astype(F32) + half_in[t, 1, i].astype(F32)
         ).astype(BF)
-        z_m(t).start()
-
-    def far_sums(t):
-        far_sum(t).wait_recv()
-        out_buf[t, 4] = (out_buf[t, 4].astype(F32) + far_in[t].astype(F32)).astype(BF)
-        half_p(t).start()
-        half_m(t).start()
+        z_m(t, i).start()
+
+    def far_sums(t, i):
+        far_sum(t, i).wait_recv()
+        out_buf[t, 4, i] = (out_buf[t, 4, i].astype(F32) + far_in[t, i].astype(F32)).astype(BF)
+        half_p(t, i).start()
+        half_m(t, i).start()
 
     def fwd_chunk(t, c):
         first = t == 0
+        second = jnp.logical_not(first)
 
         @pl.when(c == 1)
         def _():
             @pl.when(first)
             def _():
-                to_p(0).wait_recv()
-                on_p(0).start()
-                to_m(0).wait_recv()
-                on_m(0).start()
-                to_x(0).wait_recv()
-                xto_p(0).start()
-                xto_m(0).start()
+                pass_on(0)
+                for i in range(2):
+                    for o in spread(1, i):
+                        o.start()
 
             put_set(t, 1)
             put_set(t, 2)
@@ -328,40 +333,58 @@
         def _():
             @pl.when(first)
             def _():
-                on_p(0).wait_recv()
-                on_m(0).wait_recv()
-                far(0).start()
+                for i in range(2):
+                    for o in spread(1, i):
+                        o.wait_recv()
+                first_chunk(1)
+                pass_far(0)
                 for w in w_z:
                     w.wait_recv()
                 w_own[2] = w_own[1] + (w_in[1] + w_in[2] + w_in[3])
                 for w in w_y:
                     w.start()
 
-            @pl.when(jnp.logical_not(first))
+            @pl.when(second)
             def _():
-                plane_sums(0)
+                plane_sums(0, 0)
+                plane_sums(0, 1)
 
             put_set(t, 3)
             put_set(t, 4)
 
         @pl.when(c == 3)
         def _():
-            xto_p(t).wait_recv()
-            xto_m(t).wait_recv()
+            for i in range(2):
+                xto_p(t, i).wait_recv()
+                xto_m(t, i).wait_recv()
 
             @pl.when(first)
             def _():
-                for o in (to_x, to_p, to_m):
-                    o(1).start()
-
-            @pl.when(jnp.logical_not(first))
+                for i in range(2):
+                    to_p(1, i).start()
+                    to_m(1, i).start()
+
+            @pl.when(second)
             def _():
-                half_sums(0)
+                half_sums(0, 0)
+                half_sums(0, 1)
 
             put_set(t, 5)
             put_set(t, 6)
 
         forward(t, c, PC, pl.multiple_of((c - 1) * PC, PC), None)
+
+    def last_chunk(t):
+        far(t, 0).wait_recv()
+        far(t, 1).wait_recv()
+
+        @pl.when(t == 0)
+        def _():
+            to_x(1, 0).start()
+            to_x(1, 1).start()
+
+        put_set(t, 7)
+        forward(t, 4, SET, LAST_AT, None)
 
     def finish_fwd(t):
         for u in range(QPG):
@@ -383,19 +406,11 @@
 
         @pl.when((c == 3) & first)
         def _():
-            to_p(1).wait_recv()
-            on_p(1).start()
-            to_m(1).wait_recv()
-            on_m(1).start()
-            to_x(1).wait_recv()
-            xto_p(1).start()
-            xto_m(1).start()
+            pass_on(1)
 
         @pl.when((c == 1) & first)
         def _():
-            on_p(1).wait_recv()
-            on_m(1).wait_recv()
-            far(1).start()
+            pass_far(1)
 
         backward(t, c, PC, pl.multiple_of((c - 1) * PC, PC), lambda r: sets[t, 2 * c - 1 + r // SET, 1])
         put_out(t, 2 * c - 1, 0)
@@ -403,12 +418,17 @@
 
         @pl.when(c == 3)
         def _():
-            plane_p(t).start()
-            plane_m(t).start()
+            for i in range(2):
+                plane_p(t, i).start()
+                plane_m(t, i).start()
+
+        @pl.when(c == 2)
+        def _():
+            far_sums(t, 0)
 
         @pl.when(c == 1)
         def _():
-            far_sums(t)
+            far_sums(t, 1)
 
     def own_chunk(t):
         backward(t, 0, PC, OWN_AT, lambda r: sets[t, 0, 1] if r == 0 else r_kv[1, t])
@@ -422,13 +442,12 @@
 
     def both(t, _):
         lax.fori_loop(1, 4, lambda c, _: (fwd_chunk(t, c), 0)[1], 0)
-        far(t).wait_recv()
-        put_set(t, 7)
-        forward(t, 4, SET, LAST_AT, None)
+        last_chunk(t)
         finish_fwd(t)
         backward(t, 4, SET, LAST_AT, lambda r: sets[t, 7, 1])
         put_out(t, 7, 0)
-        far_sum(t).start()
+        far_sum(t, 0).start()
+        far_sum(t, 1).start()
         lax.fori_loop(0, 3, lambda i, _: (bwd_chunk(t, 3 - i), 0)[1], 0)
         return 0
 
@@ -441,19 +460,23 @@
     weight = (8192.0 / count)[0:1, :]
     w2 = cat([weight, weight], 1)
 
-    own_chunk(1)
-    plane_sums(1)
-    half_sums(1)
-    own_chunk(0)
-    owner_sum(0)
-
     def dq_copy(i):
         return pltpu.make_async_copy(p_ref.at[i, 0:256, :], dq_hbm.at[:, pair(i)], ls.at[8 + i])
 
-    for t in range(2):
+    def finish_queries(t):
         query_sums(t)
         for i in range(t * 4, t * 4 + 4):
             dq_copy(i).start()
+
+    plane_sums(1, 0)
+    own_chunk(1)
+    half_sums(1, 0)
+    plane_sums(1, 1)
+    finish_queries(1)
+    half_sums(1, 1)
+    own_chunk(0)
+    owner_sum(0)
+    finish_queries(0)
     owner_sum(1)
 
     mine = lax.broadcasted_iota(jnp.int32, (64, HD), 0) + (kv * 8 + grp) * 64 < plen
@@ -463,14 +486,16 @@
             if d == 0:
                 got_k, got_v = own[t, 0, my_rows, :], own[t, 1, my_rows, :]
             else:
-                to_owner(t, d).wait_recv()
+                to_owner(t, 0, d).wait_recv()
+                to_owner(t, 1, d).wait_recv()
                 got_k, got_v = fin[t, d, 0], fin[t, d, 1]
             dpk_ref[:, cols] = jnp.where(mine, got_k.astype(F32) * (weight * SCALE), 0.0)
             dpv_ref[:, cols] = jnp.where(mine, got_v.astype(F32) * weight, 0.0)
 
     for t in range(2):
-        for c in spread(t) + [g(t) for g in gather] + [s(t) for s in sums] + [to_owner(t, d) for d in (1, 2, 3)]:
-            c.wait_send()
+        for i in range(2):
+            for c in spread(t, i) + [g(t, i) for g in gather + sums] + [to_owner(t, i, d) for d in (1, 2, 3)]:
+                c.wait_send()
     for c in [w_x] + w_z + w_y:
         c.wait_send()
     for i in range(8):
@@ -479,12 +504,25 @@
 
 
 def hand_over(*refs):
-    n = len(refs) // 2
-    sems = refs[-1]
-    copies = [pltpu.make_async_copy(refs[i], refs[n + i], sems.at[i]) for i in range(n)]
-    for c in copies:
+    ins, outs, held, (in_sem, out_sem) = refs[0:6], refs[6:12], refs[12:18], refs[18:]
+    pieces = []
+    for i in range(6):
+        parts = 4 if i < 2 else 1
+        rows = ins[i].shape[0] // parts
+        for j in range(parts):
+            pieces.append((i, pl.ds(j * rows, rows)))
+    into = [
+        pltpu.make_async_copy(ins[i].at[r], held[i].at[r], in_sem.at[n]) for n, (i, r) in enumerate(pieces)
+    ]
+    out = [
+        pltpu.make_async_copy(held[i].at[r], outs[i].at[r], out_sem.at[n]) for n, (i, r) in enumerate(pieces)
+    ]
+    for c in into:
         c.start()
-    for c in copies:
+    for a, b in zip(into, out):
+        a.wait()
+        b.start()
+    for c in out:
         c.wait()
 
 
@@ -538,8 +576,8 @@
             pltpu.VMEM((2, 4, 2, 64, HD), BF),
             pltpu.VMEM((3, 8, 128), F32),
             pltpu.VMEM((7, 8, 128), F32),
-            dma((24,)), dma((2, 6)), dma((2, 6)), dma((2, 8)), dma((2, 8)), dma((2, 8)), dma((2, 8)),
-            dma((2, 4)), dma((2, 4)), dma((7,)), dma((7,)),
+            dma((24,)), dma((2, 2, 4)), dma((2, 2, 4)), dma((2, 2, 8)), dma((2, 2, 8)), dma((2, 2, 8)), dma((2, 2, 8)),
+            dma((2, 2, 4)), dma((2, 2, 4)), dma((7,)), dma((7,)),
         ],
         compiler_params=pltpu.CompilerParams(
             collective_id=0, has_side_effects=True, vmem_limit_bytes=62 * 2**20
@@ -553,9 +591,9 @@
     attended, grad_q, grad_rk, grad_rv, grad_pk, grad_pv = pl.pallas_call(
         hand_over,
         out_shape=shapes,
-        in_specs=[vm] * 6,
+        in_specs=[hbm] * 6,
         out_specs=[hbm] * 6,
-        scratch_shapes=[dma((6,))],
+        scratch_shapes=[pltpu.VMEM(a.shape, a.dtype) for a in shapes] + [dma((12,)), dma((12,))],
         name="hand_over",
     )(*outs)
     return (

time: 70.1 us -> 70.3 us (level)
    pallas_call x1, Pallas kernels: 64.5 us -> 65.3 us  [on_device(): pl.pallas_call(kernel, out_shape=shapes, in_specs=[sm, sm] + [hbm] * 6, o...]
where the time goes in v5:
time: 70.3 us; the launch traced here: 70.1 us
  Pallas kernels  68 us (97%)
  between operations  2.09 us (3%)
    pallas_call x1, Pallas kernels, on_device(): pl.pallas_call(kernel, out_shape=shapes, in_specs=[sm, sm] + [hbm] * 6, o...  65.3 us
    pallas_call x1, Pallas kernels, on_device(): pl.pallas_call(hand_over, out_shape=shapes, in_specs=[hbm] * 6, out_specs...  2.73 us

profile of v5, /device:TPU:1, one launch (start us, length us, event | category | flops | bytes accessed | tf_op | source)
XLA Modules:
  0.0 70.1 jit_solution(15492058329433543586)
XLA Ops:
  1.9 65.3 %attention.1 = (bf16[256,2048]{1,0:T(8,128)(2,1)}, bf16[256,2048]{1,0:T(8,128)(2,1)}, bf16[256,256]{1,0:T(8,128)(2,1)}, bf16[256,256]{1,0:T(8,128)(2,1)}, f32[64,1024]{1,0:T(8,128)}, /*index=5*/f32[64,1024]{1,0:T(8,128)}) custom-call(s32[1,1]{1,0:T(1,128)S(6)} %copy.14.rl_ref, s32[1]{0:T(128)S(6)} %copy.15.pl_ref, bf16[256,2048]{1,0:T(8,128)(2,1)} %bitcast.12, ...), custom_call_target="tpu_custom_call" | custom-call | tf_op jit(solution)/shard_map/attention/pallas_call | solution.py:541
  67.2 2.7 %hand_over.1 = (bf16[256,2048]{1,0:T(8,128)(2,1)}, bf16[256,2048]{1,0:T(8,128)(2,1)}, bf16[256,256]{1,0:T(8,128)(2,1)}, bf16[256,256]{1,0:T(8,128)(2,1)}, f32[64,1024]{1,0:T(8,128)}, /*index=5*/f32[64,1024]{1,0:T(8,128)}) custom-call(bf16[256,2048]{1,0:T(8,128)(2,1)} %get-tuple-element.18.refs_0_, bf16[256,2048]{1,0:T(8,128)(2,1)} %get-tuple-element.19.refs_1_, ...), custom_call_target="tpu_custom_call" | custom-call | tf_op jit(solution)/shard_map/hand_over/pallas_call | solution.py:591

commit v6 on v5

--- a/solution.py
+++ b/solution.py
@@ -80,6 +80,7 @@
             src_ref=src, dst_ref=dst, send_sem=ssem, recv_sem=rsem, device_id=dev, device_id_type=MESH
         )
 
+    whole = slice(None)
     def spread(t, i):
         ref = (pk_hbm, pv_hbm)[i]
         return [
@@ -91,6 +92,11 @@
     lo, hi = pl.ds(0, 128), pl.ds(128, 128)
 
     def moved(t, i, n, src, dst, dev, rows=None):
+        if i is None:
+            a, b = sets.at[t, src], sets.at[t, dst]
+            if rows is not None:
+                a, b = a.at[:, rows], b.at[:, rows]
+            return cp(a, b, gs.at[t, 0, n], gr.at[t, 0, n], dev)
         a, b = sets.at[t, src, i], sets.at[t, dst, i]
         if rows is not None:
             a, b = a.at[rows], b.at[rows]
@@ -109,16 +115,19 @@
     w_z = [cp(w_own.at[1], w_in.at[d], ws.at[d], wr.at[d], zat(d)) for d in (1, 2, 3)]
     w_y = [cp(w_own.at[2], w_in.at[3 + d], ws.at[3 + d], wr.at[3 + d], yat(d)) for d in (1, 2, 3)]
     def summed(t, i, n, src, dst, dev):
+        if i is not None:
+            src, dst = src.at[i], dst.at[i]
+        i = i or 0
         return cp(src, dst, hs.at[t, i, n], hr.at[t, i, n], dev)
 
-    far_sum = lambda t, i: summed(t, i, 0, out_buf.at[t, 7, i], far_in.at[t, i], xp)
-    half_p = lambda t, i: summed(t, i, 1, out_buf.at[t, 4, i, :, lo], half_in.at[t, 0, i], zp)
-    half_m = lambda t, i: summed(t, i, 2, out_buf.at[t, 4, i, :, hi], half_in.at[t, 1, i], zm)
-    plane_p = lambda t, i: summed(t, i, 3, out_buf.at[t, 5, i], plane_in.at[t, 0, i], zp)
-    plane_m = lambda t, i: summed(t, i, 4, out_buf.at[t, 6, i], plane_in.at[t, 1, i], zm)
-    z_p = lambda t, i: summed(t, i, 5, out_buf.at[t, 2, i], z_in.at[t, 0, i], zp)
-    z_m = lambda t, i: summed(t, i, 6, out_buf.at[t, 1, i], z_in.at[t, 1, i], zm)
-    x_sum = lambda t, i: summed(t, i, 7, out_buf.at[t, 3, i], x_in.at[t, i], xp)
+    far_sum = lambda t, i: summed(t, i, 0, out_buf.at[t, 7], far_in.at[t], xp)
+    half_p = lambda t, i: summed(t, i, 1, out_buf.at[t, 4, :, :, lo], half_in.at[t, 0], zp)
+    half_m = lambda t, i: summed(t, i, 2, out_buf.at[t, 4, :, :, hi], half_in.at[t, 1], zm)
+    plane_p = lambda t, i: summed(t, i, 3, out_buf.at[t, 5], plane_in.at[t, 0], zp)
+    plane_m = lambda t, i: summed(t, i, 4, out_buf.at[t, 6], plane_in.at[t, 1], zm)
+    z_p = lambda t, i: summed(t, i, 5, out_buf.at[t, 2], z_in.at[t, 0], zp)
+    z_m = lambda t, i: summed(t, i, 6, out_buf.at[t, 1], z_in.at[t, 1], zm)
+    x_sum = lambda t, i: summed(t, i, 7, out_buf.at[t, 3], x_in.at[t], xp)
     sums = [far_sum, half_p, half_m, plane_p, plane_m, z_p, z_m, x_sum]
 
     def to_owner(t, i, d):
@@ -174,36 +183,48 @@
 
     def scores(t, j, u, rows, at, mask):
         h = t * QPG + u
-        s_ref = s_bufs[u % 2]
         top = None
         for r in range(0, rows, 256):
             s = dot(k_n[t, pl.ds(at + r, 256), :], q_t[h], NN) * (SCALE * LOG2E)
             if mask is not None and r:
                 s = jnp.where(mask, s, -1e30)
-            s_ref[r:r + 256, :] = s
+            s_bufs[u % 2][r:r + 256, :] = s
             b = jnp.max(s.reshape(32, 8, SLOTS), 0)
             top = b if top is None else jnp.maximum(top, b)
+            yield
         m = jnp.max(top, 0, keepdims=True)
         mc[j, h] = m if mask is not None else jnp.maximum(mc[j - 1, h], m)
 
+    def weights(t, j, u, rows, at):
+        h = t * QPG + u
+        m = mc[j, h]
+        for r in range(0, rows, 256):
+            p = jnp.exp2(s_bufs[u % 2][r:r + 256, :] - m).astype(BF)
+            p_ref[h, pl.ds(at + r, 256), :] = p
+            ds_bufs[u % 2][r:r + 256, :] = p
+            yield
+
     def attend(t, j, u, rows, at, first):
         h = t * QPG + u
-        s_ref = s_bufs[u % 2]
-        m = mc[j, h]
-        parts = []
-        for r in range(0, rows, 256):
-            p = jnp.exp2(s_ref[r:r + 256, :] - m).astype(BF)
-            p_ref[h, pl.ds(at + r, 256), :] = p
-            parts.append(p)
-        new = dot(v_t[t, :, pl.ds(at, rows)], cat(parts, 0), NN)
-        o_acc[h] = new if first else o_acc[h] * jnp.exp2(mc[j - 1, h] - m) + new
+        new = dot(v_t[t, :, pl.ds(at, rows)], ds_bufs[u % 2][0:rows, :], NN)
+        yield
+        o_acc[h] = new if first else o_acc[h] * jnp.exp2(mc[j - 1, h] - mc[j, h]) + new
 
     def forward(t, j, rows, at, mask):
-        for u in range(QPG + 1):
+        for u in range(QPG + 2):
+            steps = []
             if u < QPG:
-                scores(t, j, u, rows, at, mask)
-            if u > 0:
-                attend(t, j, u - 1, rows, at, mask is not None)
+                steps.append(scores(t, j, u, rows, at, mask))
+            if 0 <= u - 1 < QPG:
+                steps.append(weights(t, j, u - 1, rows, at))
+            if 0 <= u - 2:
+                steps.append(attend(t, j, u - 2, rows, at, mask is not None))
+            while steps:
+                for step in list(steps):
+                    try:
+                        next(step)
+                    except StopIteration:
+                        steps.remove(step)
 
     def weigh(t, j, u, rows, at, values):
         h = t * QPG + u
@@ -261,8 +282,8 @@
     for c in w_z:
         c.start()
 
-    def pass_on(t):
-        for i in range(2):
+    def pass_on(t, parts):
+        for i in parts:
             to_p(t, i).wait_recv()
             on_p(t, i).start()
             to_m(t, i).wait_recv()
@@ -271,45 +292,46 @@
             xto_p(t, i).start()
             xto_m(t, i).start()
 
-    def pass_far(t):
-        for i in range(2):
+    def pass_far(t, parts):
+        for i in parts:
             on_p(t, i).wait_recv()
             on_m(t, i).wait_recv()
             far(t, i).start()
 
-    def owner_sum(t):
-        for i in range(2):
-            z_p(t, i).wait_recv()
-            z_m(t, i).wait_recv()
-            x_sum(t, i).wait_recv()
-            total = out_buf[t, 0, i].astype(F32) + z_in[t, 0, i].astype(F32)
-            total = total + (z_in[t, 1, i].astype(F32) + x_in[t, i].astype(F32))
-            own[t, i] = total.astype(BF).T
+    def owner_sum(t, i):
+        z_p(t, i).wait_recv()
+        z_m(t, i).wait_recv()
+        x_sum(t, i).wait_recv()
+        for n in (0, 1) if i is None else (i,):
+            total = out_buf[t, 0, n].astype(F32) + z_in[t, 0, n].astype(F32)
+            total = total + (z_in[t, 1, n].astype(F32) + x_in[t, n].astype(F32))
+            own[t, n] = total.astype(BF).T
             for d in (1, 2, 3):
-                to_owner(t, i, d).start()
+                to_owner(t, n, d).start()
+
+    def add_to(ref, more):
+        ref[...] = (ref[...].astype(F32) + more).astype(BF)
 
     def plane_sums(t, i):
+        n = whole if i is None else i
         plane_p(t, i).wait_recv()
         plane_m(t, i).wait_recv()
-        total = plane_in[t, 0, i].astype(F32) + plane_in[t, 1, i].astype(F32)
-        out_buf[t, 3, i] = (out_buf[t, 3, i].astype(F32) + total).astype(BF)
+        add_to(out_buf.at[t, 3, n], plane_in[t, 0, n].astype(F32) + plane_in[t, 1, n].astype(F32))
         x_sum(t, i).start()
 
     def half_sums(t, i):
+        n = whole if i is None else i
         half_p(t, i).wait_recv()
-        out_buf[t, 2, i, :, 0:128] = (
-            out_buf[t, 2, i, :, 0:128].astype(F32) + half_in[t, 0, i].astype(F32)
-        ).astype(BF)
+        add_to(out_buf.at[t, 2, n, :, 0:128], half_in[t, 0, n].astype(F32))
         z_p(t, i).start()
         half_m(t, i).wait_recv()
-        out_buf[t, 1, i, :, 128:256] = (
-            out_buf[t, 1, i, :, 128:256].astype(F32) + half_in[t, 1, i].astype(F32)
-        ).astype(BF)
+        add_to(out_buf.at[t, 1, n, :, 128:256], half_in[t, 1, n].astype(F32))
         z_m(t, i).start()
 
     def far_sums(t, i):
+        n = whole if i is None else i
         far_sum(t, i).wait_recv()
-        out_buf[t, 4, i] = (out_buf[t, 4, i].astype(F32) + far_in[t, i].astype(F32)).astype(BF)
+        add_to(out_buf.at[t, 4, n], far_in[t, n].astype(F32))
         half_p(t, i).start()
         half_m(t, i).start()
 
@@ -321,7 +343,7 @@
         def _():
             @pl.when(first)
             def _():
-                pass_on(0)
+                pass_on(0, (0, 1))
                 for i in range(2):
                     for o in spread(1, i):
                         o.start()
@@ -337,7 +359,7 @@
                     for o in spread(1, i):
                         o.wait_recv()
                 first_chunk(1)
-                pass_far(0)
+                pass_far(0, (0, 1))
                 for w in w_z:
                     w.wait_recv()
                 w_own[2] = w_own[1] + (w_in[1] + w_in[2] + w_in[3])
@@ -346,28 +368,26 @@
 
             @pl.when(second)
             def _():
-                plane_sums(0, 0)
-                plane_sums(0, 1)
+                plane_sums(0, None)
 
             put_set(t, 3)
             put_set(t, 4)
 
         @pl.when(c == 3)
         def _():
-            for i in range(2):
-                xto_p(t, i).wait_recv()
-                xto_m(t, i).wait_recv()
-
             @pl.when(first)
             def _():
                 for i in range(2):
-                    to_p(1, i).start()
-                    to_m(1, i).start()
+                    xto_p(0, i).wait_recv()
+                    xto_m(0, i).wait_recv()
+                to_p(1, None).start()
+                to_m(1, None).start()
 
             @pl.when(second)
             def _():
-                half_sums(0, 0)
-                half_sums(0, 1)
+                xto_p(1, None).wait_recv()
+                xto_m(1, None).wait_recv()
+                half_sums(0, None)
 
             put_set(t, 5)
             put_set(t, 6)
@@ -375,13 +395,15 @@
         forward(t, c, PC, pl.multiple_of((c - 1) * PC, PC), None)
 
     def last_chunk(t):
-        far(t, 0).wait_recv()
-        far(t, 1).wait_recv()
-
         @pl.when(t == 0)
         def _():
-            to_x(1, 0).start()
-            to_x(1, 1).start()
+            far(0, 0).wait_recv()
+            far(0, 1).wait_recv()
+            to_x(1, None).start()
+
+        @pl.when(t == 1)
+        def _():
+            far(1, None).wait_recv()
 
         put_set(t, 7)
         forward(t, 4, SET, LAST_AT, None)
@@ -403,32 +425,42 @@
 
     def bwd_chunk(t, c):
         first = t == 0
+        second = jnp.logical_not(first)
 
         @pl.when((c == 3) & first)
         def _():
-            pass_on(1)
+            pass_on(1, (None,))
 
         @pl.when((c == 1) & first)
         def _():
-            pass_far(1)
+            pass_far(1, (None,))
 
         backward(t, c, PC, pl.multiple_of((c - 1) * PC, PC), lambda r: sets[t, 2 * c - 1 + r // SET, 1])
         put_out(t, 2 * c - 1, 0)
         put_out(t, 2 * c, 1)
 
-        @pl.when(c == 3)
+        @pl.when((c == 3) & first)
+        def _():
+            plane_p(0, None).start()
+            plane_m(0, None).start()
+
+        @pl.when((c == 3) & second)
         def _():
             for i in range(2):
-                plane_p(t, i).start()
-                plane_m(t, i).start()
-
-        @pl.when(c == 2)
-        def _():
-            far_sums(t, 0)
-
-        @pl.when(c == 1)
-        def _():
-            far_sums(t, 1)
+                plane_p(1, i).start()
+                plane_m(1, i).start()
+
+        @pl.when((c == 2) & second)
+        def _():
+            far_sums(1, 0)
+
+        @pl.when((c == 1) & first)
+        def _():
+            far_sums(0, None)
+
+        @pl.when((c == 1) & second)
+        def _():
+            far_sums(1, 1)
 
     def own_chunk(t):
         backward(t, 0, PC, OWN_AT, lambda r: sets[t, 0, 1] if r == 0 else r_kv[1, t])
@@ -446,8 +478,16 @@
         finish_fwd(t)
         backward(t, 4, SET, LAST_AT, lambda r: sets[t, 7, 1])
         put_out(t, 7, 0)
-        far_sum(t, 0).start()
-        far_sum(t, 1).start()
+
+        @pl.when(t == 0)
+        def _():
+            far_sum(0, None).start()
+
+        @pl.when(t == 1)
+        def _():
+            far_sum(1, 0).start()
+            far_sum(1, 1).start()
+
         lax.fori_loop(0, 3, lambda i, _: (bwd_chunk(t, 3 - i), 0)[1], 0)
         return 0
 
@@ -468,19 +508,9 @@
         for i in range(t * 4, t * 4 + 4):
             dq_copy(i).start()
 
-    plane_sums(1, 0)
-    own_chunk(1)
-    half_sums(1, 0)
-    plane_sums(1, 1)
-    finish_queries(1)
-    half_sums(1, 1)
-    own_chunk(0)
-    owner_sum(0)
-    finish_queries(0)
-    owner_sum(1)
-
     mine = lax.broadcasted_iota(jnp.int32, (64, HD), 0) + (kv * 8 + grp) * 64 < plen
-    for t in range(2):
+
+    def finish_keys(t):
         for d in range(4):
             cols = head_cols(kvat(4 - d), t)
             if d == 0:
@@ -492,15 +522,39 @@
             dpk_ref[:, cols] = jnp.where(mine, got_k.astype(F32) * (weight * SCALE), 0.0)
             dpv_ref[:, cols] = jnp.where(mine, got_v.astype(F32) * weight, 0.0)
 
+    plane_sums(1, 0)
+    own_chunk(1)
+    half_sums(1, 0)
+    plane_sums(1, 1)
+    finish_queries(1)
+    half_sums(1, 1)
+    own_chunk(0)
+    owner_sum(0, None)
+    finish_queries(0)
+    owner_sum(1, 0)
+    finish_keys(0)
+    owner_sum(1, 1)
+
+    for c in [w_x] + w_z + w_y:
+        c.wait_send()
     for t in range(2):
         for i in range(2):
-            for c in spread(t, i) + [g(t, i) for g in gather + sums] + [to_owner(t, i, d) for d in (1, 2, 3)]:
+            for c in spread(t, i):
                 c.wait_send()
-    for c in [w_x] + w_z + w_y:
-        c.wait_send()
+        for i in ((0, 1), (None,))[t]:
+            for g in gather:
+                g(t, i).wait_send()
+        for i in ((None,), (0, 1))[t]:
+            for g in sums:
+                g(t, i).wait_send()
     for i in range(8):
         o_copy(i).wait()
         dq_copy(i).wait()
+    finish_keys(1)
+    for t in range(2):
+        for i in range(2):
+            for d in (1, 2, 3):
+                to_owner(t, i, d).wait_send()
 
 
 def hand_over(*refs):

time: 70.3 us -> 72.1 us (1.026)
  Pallas kernels: 68 us -> 69.9 us
    pallas_call x1, Pallas kernels: 65.3 us -> 67.2 us  [on_device(): pl.pallas_call(kernel, out_shape=shapes, in_specs=[sm, sm] + [hbm] * 6, o...]
where the time goes in v6:
time: 72.1 us; the launch traced here: 72 us
  Pallas kernels  69.9 us (97%)
  between operations  2.09 us (3%)
    pallas_call x1, Pallas kernels, on_device(): pl.pallas_call(kernel, out_shape=shapes, in_specs=[sm, sm] + [hbm] * 6, o...  67.2 us
    pallas_call x1, Pallas kernels, on_device(): pl.pallas_call(hand_over, out_shape=shapes, in_specs=[hbm] * 6, out_specs...  2.73 us

profile of v6, /device:TPU:1, one launch (start us, length us, event | category | flops | bytes accessed | tf_op | source)
XLA Modules:
  0.0 72.0 jit_solution(9376675462169302843)
XLA Ops:
  1.9 67.2 %attention.1 = (bf16[256,2048]{1,0:T(8,128)(2,1)}, bf16[256,2048]{1,0:T(8,128)(2,1)}, bf16[256,256]{1,0:T(8,128)(2,1)}, bf16[256,256]{1,0:T(8,128)(2,1)}, f32[64,1024]{1,0:T(8,128)}, /*index=5*/f32[64,1024]{1,0:T(8,128)}) custom-call(s32[1,1]{1,0:T(1,128)S(6)} %copy.14.rl_ref, s32[1]{0:T(128)S(6)} %copy.15.pl_ref, bf16[256,2048]{1,0:T(8,128)(2,1)} %bitcast.12, ...), custom_call_target="tpu_custom_call" | custom-call | tf_op jit(solution)/shard_map/attention/pallas_call | solution.py:595
  69.1 2.7 %hand_over.1 = (bf16[256,2048]{1,0:T(8,128)(2,1)}, bf16[256,2048]{1,0:T(8,128)(2,1)}, bf16[256,256]{1,0:T(8,128)(2,1)}, bf16[256,256]{1,0:T(8,128)(2,1)}, f32[64,1024]{1,0:T(8,128)}, /*index=5*/f32[64,1024]{1,0:T(8,128)}) custom-call(bf16[256,2048]{1,0:T(8,128)(2,1)} %get-tuple-element.18.refs_0_, bf16[256,2048]{1,0:T(8,128)(2,1)} %get-tuple-element.19.refs_1_, ...), custom_call_target="tpu_custom_call" | custom-call | tf_op jit(solution)/shard_map/hand_over/pallas_call | solution.py:645

commit v7 on v4

--- a/solution.py
+++ b/solution.py
@@ -339,7 +339,9 @@
 
             @pl.when(jnp.logical_not(first))
             def _():
-                plane_sums(0)
+                on_p(1).wait_recv()
+                on_m(1).wait_recv()
+                far(1).start()
 
             put_set(t, 3)
             put_set(t, 4)
@@ -353,10 +355,6 @@
             def _():
                 for o in (to_x, to_p, to_m):
                     o(1).start()
-
-            @pl.when(jnp.logical_not(first))
-            def _():
-                half_sums(0)
 
             put_set(t, 5)
             put_set(t, 6)
@@ -378,10 +376,11 @@
         out_buf[t, s, 0] = dk_acc[:, cols].astype(BF)
         out_buf[t, s, 1] = dv_acc[:, cols].astype(BF)
 
-    def bwd_chunk(t, c):
-        first = t == 0
-
-        @pl.when((c == 3) & first)
+    def bwd_step(t, n):
+        s = t * (1 - n % 2)
+        c = 3 - t * ((n + 1) // 2)
+
+        @pl.when(t == 0)
         def _():
             to_p(1).wait_recv()
             on_p(1).start()
@@ -391,24 +390,32 @@
             xto_p(1).start()
             xto_m(1).start()
 
-        @pl.when((c == 1) & first)
-        def _():
-            on_p(1).wait_recv()
-            on_m(1).wait_recv()
-            far(1).start()
-
-        backward(t, c, PC, pl.multiple_of((c - 1) * PC, PC), lambda r: sets[t, 2 * c - 1 + r // SET, 1])
-        put_out(t, 2 * c - 1, 0)
-        put_out(t, 2 * c, 1)
-
-        @pl.when(c == 3)
-        def _():
-            plane_p(t).start()
-            plane_m(t).start()
-
-        @pl.when(c == 1)
-        def _():
-            far_sums(t)
+        backward(s, c, PC, pl.multiple_of((c - 1) * PC, PC), lambda r: sets[s, 2 * c - 1 + r // SET, 1])
+        put_out(s, 2 * c - 1, 0)
+        put_out(s, 2 * c, 1)
+
+        @pl.when(n == 0)
+        def _():
+            plane_p(s).start()
+            plane_m(s).start()
+
+        @pl.when(n == 1)
+        def _():
+            far_sums(0)
+            plane_sums(0)
+
+        @pl.when(n == 2)
+        def _():
+            far_sums(1)
+
+        @pl.when(n == 3)
+        def _():
+            half_sums(0)
+            plane_sums(1)
+
+        @pl.when(n == 4)
+        def _():
+            half_sums(1)
 
     def own_chunk(t):
         backward(t, 0, PC, OWN_AT, lambda r: sets[t, 0, 1] if r == 0 else r_kv[1, t])
@@ -429,7 +436,7 @@
         backward(t, 4, SET, LAST_AT, lambda r: sets[t, 7, 1])
         put_out(t, 7, 0)
         far_sum(t).start()
-        lax.fori_loop(0, 3, lambda i, _: (bwd_chunk(t, 3 - i), 0)[1], 0)
+        lax.fori_loop(0, 1 + 4 * t, lambda n, _: (bwd_step(t, n), 0)[1], 0)
         return 0
 
     lax.fori_loop(0, 2, both, 0)
@@ -441,20 +448,20 @@
     weight = (8192.0 / count)[0:1, :]
     w2 = cat([weight, weight], 1)
 
-    own_chunk(1)
-    plane_sums(1)
-    half_sums(1)
-    own_chunk(0)
-    owner_sum(0)
-
     def dq_copy(i):
         return pltpu.make_async_copy(p_ref.at[i, 0:256, :], dq_hbm.at[:, pair(i)], ls.at[8 + i])
 
-    for t in range(2):
+    def finish_queries(t):
         query_sums(t)
         for i in range(t * 4, t * 4 + 4):
             dq_copy(i).start()
+
+    own_chunk(1)
+    own_chunk(0)
+    owner_sum(0)
+    finish_queries(1)
     owner_sum(1)
+    finish_queries(0)
 
     mine = lax.broadcasted_iota(jnp.int32, (64, HD), 0) + (kv * 8 + grp) * 64 < plen
     for t in range(2):
@@ -479,12 +486,25 @@
 
 
 def hand_over(*refs):
-    n = len(refs) // 2
-    sems = refs[-1]
-    copies = [pltpu.make_async_copy(refs[i], refs[n + i], sems.at[i]) for i in range(n)]
-    for c in copies:
+    ins, outs, held, (in_sem, out_sem) = refs[0:6], refs[6:12], refs[12:18], refs[18:]
+    pieces = []
+    for i in range(6):
+        parts = 4 if i < 2 else 1
+        rows = ins[i].shape[0] // parts
+        for j in range(parts):
+            pieces.append((i, pl.ds(j * rows, rows)))
+    into = [
+        pltpu.make_async_copy(ins[i].at[r], held[i].at[r], in_sem.at[n]) for n, (i, r) in enumerate(pieces)
+    ]
+    out = [
+        pltpu.make_async_copy(held[i].at[r], outs[i].at[r], out_sem.at[n]) for n, (i, r) in enumerate(pieces)
+    ]
+    for c in into:
         c.start()
-    for c in copies:
+    for a, b in zip(into, out):
+        a.wait()
+        b.start()
+    for c in out:
         c.wait()
 
 
@@ -553,9 +573,9 @@
     attended, grad_q, grad_rk, grad_rv, grad_pk, grad_pv = pl.pallas_call(
         hand_over,
         out_shape=shapes,
-        in_specs=[vm] * 6,
+        in_specs=[hbm] * 6,
         out_specs=[hbm] * 6,
-        scratch_shapes=[dma((6,))],
+        scratch_shapes=[pltpu.VMEM(a.shape, a.dtype) for a in shapes] + [dma((12,)), dma((12,))],
         name="hand_over",
     )(*outs)
     return (

time: 70.1 us -> 66.6 us (0.950)
  Pallas kernels: 67.8 us -> 64.4 us
    pallas_call x1, Pallas kernels: 64.5 us -> 61.7 us  [on_device(): pl.pallas_call(kernel, out_shape=shapes, in_specs=[sm, sm] + [hbm] * 6, o...]
where the time goes in v7:
time: 66.6 us; the launch traced here: 66.5 us
  Pallas kernels  64.4 us (97%)
  between operations  2.09 us (3%)
    pallas_call x1, Pallas kernels, on_device(): pl.pallas_call(kernel, out_shape=shapes, in_specs=[sm, sm] + [hbm] * 6, o...  61.7 us
    pallas_call x1, Pallas kernels, on_device(): pl.pallas_call(hand_over, out_shape=shapes, in_specs=[hbm] * 6, out_specs...  2.73 us

profile of v7, /device:TPU:1, one launch (start us, length us, event | category | flops | bytes accessed | tf_op | source)
XLA Modules:
  0.0 66.5 jit_solution(2834220738664169607)
XLA Ops:
  1.9 61.7 %attention.1 = (bf16[256,2048]{1,0:T(8,128)(2,1)}, bf16[256,2048]{1,0:T(8,128)(2,1)}, bf16[256,256]{1,0:T(8,128)(2,1)}, bf16[256,256]{1,0:T(8,128)(2,1)}, f32[64,1024]{1,0:T(8,128)}, /*index=5*/f32[64,1024]{1,0:T(8,128)}) custom-call(s32[1,1]{1,0:T(1,128)S(6)} %copy.14.rl_ref, s32[1]{0:T(128)S(6)} %copy.15.pl_ref, bf16[256,2048]{1,0:T(8,128)(2,1)} %bitcast.12, ...), custom_call_target="tpu_custom_call" | custom-call | tf_op jit(solution)/shard_map/attention/pallas_call | solution.py:523
  63.6 2.7 %hand_over.1 = (bf16[256,2048]{1,0:T(8,128)(2,1)}, bf16[256,2048]{1,0:T(8,128)(2,1)}, bf16[256,256]{1,0:T(8,128)(2,1)}, bf16[256,256]{1,0:T(8,128)(2,1)}, f32[64,1024]{1,0:T(8,128)}, /*index=5*/f32[64,1024]{1,0:T(8,128)}) custom-call(bf16[256,2048]{1,0:T(8,128)(2,1)} %get-tuple-element.18.refs_0_, bf16[256,2048]{1,0:T(8,128)(2,1)} %get-tuple-element.19.refs_1_, ...), custom_call_target="tpu_custom_call" | custom-call | tf_op jit(solution)/shard_map/hand_over/pallas_call | solution.py:573

commit v8 on v7

--- a/solution.py
+++ b/solution.py
@@ -176,36 +176,48 @@
 
     def scores(t, j, u, rows, at, mask):
         h = t * QPG + u
-        s_ref = s_bufs[u % 2]
         top = None
         for r in range(0, rows, 256):
             s = dot(k_n[t, pl.ds(at + r, 256), :], q_t[h], NN) * (SCALE * LOG2E)
             if mask is not None and r:
                 s = jnp.where(mask, s, -1e30)
-            s_ref[r:r + 256, :] = s
+            s_bufs[u % 2][r:r + 256, :] = s
             b = jnp.max(s.reshape(32, 8, SLOTS), 0)
             top = b if top is None else jnp.maximum(top, b)
+            yield
         m = jnp.max(top, 0, keepdims=True)
         mc[j, h] = m if mask is not None else jnp.maximum(mc[j - 1, h], m)
 
+    def weights(t, j, u, rows, at):
+        h = t * QPG + u
+        m = mc[j, h]
+        for r in range(0, rows, 256):
+            p = jnp.exp2(s_bufs[u % 2][r:r + 256, :] - m).astype(BF)
+            p_ref[h, pl.ds(at + r, 256), :] = p
+            ds_bufs[u % 2][r:r + 256, :] = p
+            yield
+
     def attend(t, j, u, rows, at, first):
         h = t * QPG + u
-        s_ref = s_bufs[u % 2]
-        m = mc[j, h]
-        parts = []
-        for r in range(0, rows, 256):
-            p = jnp.exp2(s_ref[r:r + 256, :] - m).astype(BF)
-            p_ref[h, pl.ds(at + r, 256), :] = p
-            parts.append(p)
-        new = dot(v_t[t, :, pl.ds(at, rows)], cat(parts, 0), NN)
-        o_acc[h] = new if first else o_acc[h] * jnp.exp2(mc[j - 1, h] - m) + new
+        new = dot(v_t[t, :, pl.ds(at, rows)], ds_bufs[u % 2][0:rows, :], NN)
+        yield
+        o_acc[h] = new if first else o_acc[h] * jnp.exp2(mc[j - 1, h] - mc[j, h]) + new
 
     def forward(t, j, rows, at, mask):
-        for u in range(QPG + 1):
+        for u in range(QPG + 2):
+            steps = []
             if u < QPG:
-                scores(t, j, u, rows, at, mask)
-            if u > 0:
-                attend(t, j, u - 1, rows, at, mask is not None)
+                steps.append(scores(t, j, u, rows, at, mask))
+            if 0 <= u - 1 < QPG:
+                steps.append(weights(t, j, u - 1, rows, at))
+            if 0 <= u - 2:
+                steps.append(attend(t, j, u - 2, rows, at, mask is not None))
+            while steps:
+                for step in list(steps):
+                    try:
+                        next(step)
+                    except StopIteration:
+                        steps.remove(step)
 
     def weigh(t, j, u, rows, at, values):
         h = t * QPG + u
@@ -489,7 +501,7 @@
     ins, outs, held, (in_sem, out_sem) = refs[0:6], refs[6:12], refs[12:18], refs[18:]
     pieces = []
     for i in range(6):
-        parts = 4 if i < 2 else 1
+        parts = 8 if i < 2 else 1
         rows = ins[i].shape[0] // parts
         for j in range(parts):
             pieces.append((i, pl.ds(j * rows, rows)))
@@ -575,7 +587,7 @@
         out_shape=shapes,
         in_specs=[hbm] * 6,
         out_specs=[hbm] * 6,
-        scratch_shapes=[pltpu.VMEM(a.shape, a.dtype) for a in shapes] + [dma((12,)), dma((12,))],
+        scratch_shapes=[pltpu.VMEM(a.shape, a.dtype) for a in shapes] + [dma((20,)), dma((20,))],
         name="hand_over",
     )(*outs)
     return (

time: 66.6 us -> 67.1 us (level)
  no operation moved by 1% of the time
where the time goes in v8:
time: 67.1 us; the launch traced here: 67 us
  Pallas kernels  64.9 us (97%)
  between operations  2.09 us (3%)
    pallas_call x1, Pallas kernels, on_device(): pl.pallas_call(kernel, out_shape=shapes, in_specs=[sm, sm] + [hbm] * 6, o...  61.9 us
    pallas_call x1, Pallas kernels, on_device(): pl.pallas_call(hand_over, out_shape=shapes, in_specs=[hbm] * 6, out_specs...  2.99 us

profile of v8, /device:TPU:1, one launch (start us, length us, event | category | flops | bytes accessed | tf_op | source)
XLA Modules:
  0.0 67.0 jit_solution(14838060262579355863)
XLA Ops:
  1.9 61.9 %attention.1 = (bf16[256,2048]{1,0:T(8,128)(2,1)}, bf16[256,2048]{1,0:T(8,128)(2,1)}, bf16[256,256]{1,0:T(8,128)(2,1)}, bf16[256,256]{1,0:T(8,128)(2,1)}, f32[64,1024]{1,0:T(8,128)}, /*index=5*/f32[64,1024]{1,0:T(8,128)}) custom-call(s32[1,1]{1,0:T(1,128)S(6)} %copy.14.rl_ref, s32[1]{0:T(128)S(6)} %copy.15.pl_ref, bf16[256,2048]{1,0:T(8,128)(2,1)} %bitcast.12, ...), custom_call_target="tpu_custom_call" | custom-call | tf_op jit(solution)/shard_map/attention/pallas_call | solution.py:535
  63.8 3.0 %hand_over.1 = (bf16[256,2048]{1,0:T(8,128)(2,1)}, bf16[256,2048]{1,0:T(8,128)(2,1)}, bf16[256,256]{1,0:T(8,128)(2,1)}, bf16[256,256]{1,0:T(8,128)(2,1)}, f32[64,1024]{1,0:T(8,128)}, /*index=5*/f32[64,1024]{1,0:T(8,128)}) custom-call(bf16[256,2048]{1,0:T(8,128)(2,1)} %get-tuple-element.18.refs_0_, bf16[256,2048]{1,0:T(8,128)(2,1)} %get-tuple-element.19.refs_1_, ...), custom_call_target="tpu_custom_call" | custom-call | tf_op jit(solution)/shard_map/hand_over/pallas_call | solution.py:585

commit v9 on v8

--- a/solution.py
+++ b/solution.py
@@ -501,7 +501,7 @@
     ins, outs, held, (in_sem, out_sem) = refs[0:6], refs[6:12], refs[12:18], refs[18:]
     pieces = []
     for i in range(6):
-        parts = 8 if i < 2 else 1
+        parts = 2 if i < 2 else 1
         rows = ins[i].shape[0] // parts
         for j in range(parts):
             pieces.append((i, pl.ds(j * rows, rows)))
@@ -587,7 +587,7 @@
         out_shape=shapes,
         in_specs=[hbm] * 6,
         out_specs=[hbm] * 6,
-        scratch_shapes=[pltpu.VMEM(a.shape, a.dtype) for a in shapes] + [dma((20,)), dma((20,))],
+        scratch_shapes=[pltpu.VMEM(a.shape, a.dtype) for a in shapes] + [dma((8,)), dma((8,))],
         name="hand_over",
     )(*outs)
     return (

time: 67.1 us -> 66.9 us (level)
  no operation moved by 1% of the time
where the time goes in v9:
time: 66.9 us; the launch traced here: 66.7 us
  Pallas kernels  64.6 us (97%)
  between operations  2.09 us (3%)
    pallas_call x1, Pallas kernels, on_device(): pl.pallas_call(kernel, out_shape=shapes, in_specs=[sm, sm] + [hbm] * 6, o...  61.9 us
    pallas_call x1, Pallas kernels, on_device(): pl.pallas_call(hand_over, out_shape=shapes, in_specs=[hbm] * 6, out_specs...  2.75 us

profile of v9, /device:TPU:1, one launch (start us, length us, event | category | flops | bytes accessed | tf_op | source)
XLA Modules:
  0.0 66.7 jit_solution(5849652973891221733)
XLA Ops:
  1.9 61.9 %attention.1 = (bf16[256,2048]{1,0:T(8,128)(2,1)}, bf16[256,2048]{1,0:T(8,128)(2,1)}, bf16[256,256]{1,0:T(8,128)(2,1)}, bf16[256,256]{1,0:T(8,128)(2,1)}, f32[64,1024]{1,0:T(8,128)}, /*index=5*/f32[64,1024]{1,0:T(8,128)}) custom-call(s32[1,1]{1,0:T(1,128)S(6)} %copy.14.rl_ref, s32[1]{0:T(128)S(6)} %copy.15.pl_ref, bf16[256,2048]{1,0:T(8,128)(2,1)} %bitcast.12, ...), custom_call_target="tpu_custom_call" | custom-call | tf_op jit(solution)/shard_map/attention/pallas_call | solution.py:535
  63.8 2.7 %hand_over.1 = (bf16[256,2048]{1,0:T(8,128)(2,1)}, bf16[256,2048]{1,0:T(8,128)(2,1)}, bf16[256,256]{1,0:T(8,128)(2,1)}, bf16[256,256]{1,0:T(8,128)(2,1)}, f32[64,1024]{1,0:T(8,128)}, /*index=5*/f32[64,1024]{1,0:T(8,128)}) custom-call(bf16[256,2048]{1,0:T(8,128)(2,1)} %get-tuple-element.18.refs_0_, bf16[256,2048]{1,0:T(8,128)(2,1)} %get-tuple-element.19.refs_1_, ...), custom_call_target="tpu_custom_call" | custom-call | tf_op jit(solution)/shard_map/hand_over/pallas_call | solution.py:585
